TPU v7x, 256 devices: a whole 4x4x8 slice. The times are simulated.
256 devices in a mesh: lon: 16 (over y, x_lo, core), lat: 16 (over x_hi, z).
Axes of the slice: x: 4 (x_hi: 2, x_lo: 2; x = x_hi * 2 + x_lo), y: 4, z: 8, core: 2. Of those that a mesh axis runs over, the one named last changes fastest.
Arguments:
- fields: bfloat16 [1024, 64, 512], P('lon', 'lat'), may hold values from -12 to 12
- in_weight: bfloat16 [512, 1536], replicated, may hold values from -1 to 1
- out_weight: bfloat16 [512, 512], replicated, may hold values from -0.25 to 0.25
- cotangent: bfloat16 [1024, 64, 512], P('lon', 'lat'), may hold values from -6 to 6
Outputs:
- grad_fields: bfloat16 [1024, 64, 512], P('lon', 'lat')
All inputs are finite; a program needn't handle non-finite values.
Results may differ from a plain program's by a relative error of at most 0.034.
Values may be sent and summed in bfloat16 or wider, within the bound.
A program may use at most 128 MiB of HBM per device.

v0:
```python
import math

import jax
import jax.numpy as jnp
from jax import lax
from jax.sharding import PartitionSpec as P

HEADS = 8


def split_heads(array, head_count):
    return array.reshape(array.shape[0], array.shape[1], head_count, array.shape[2] // head_count)


def attention_grads(query, keys, values, grad_out, temper, layout):
    key_layout = layout.replace("s", "t")
    scores = (
        jnp.einsum(
            layout + "," + key_layout + "->bhst", query, keys, preferred_element_type=jnp.float32
        )
        * temper
    )
    maxima = jnp.max(scores, axis=-1, keepdims=True)
    expos = jnp.exp(scores - maxima)
    totals = jnp.sum(expos, axis=-1, keepdims=True)
    weights = expos / totals
    weights_bf = weights.astype(jnp.bfloat16)
    output = jnp.einsum(
        "bhst," + key_layout + "->" + layout, weights_bf, values, preferred_element_type=jnp.float32
    ).astype(jnp.bfloat16)
    deltas = jnp.einsum(
        layout + "," + layout + "->bhs", grad_out, output, preferred_element_type=jnp.float32
    )
    grad_prob = jnp.einsum(
        layout + "," + key_layout + "->bhst", grad_out, values, preferred_element_type=jnp.float32
    )
    grad_score = (weights * (grad_prob - deltas[..., None])).astype(jnp.bfloat16)
    grad_query = (
        jnp.einsum(
            "bhst," + key_layout + "->" + layout,
            grad_score,
            keys,
            preferred_element_type=jnp.float32,
        )
        * temper
    )
    log_total = maxima[..., 0] + jnp.log(totals[..., 0])
    return (grad_query, grad_score, weights_bf, log_total, deltas)


def per_device(fields, in_weight, out_weight, cotangent):
    lon_rows, lat_rows, width = fields.shape
    head_count = HEADS // 2
    half_width = width // 2
    head_size = width // HEADS
    temper = 1.0 / math.sqrt(head_size)
    qkv = jnp.dot(fields.reshape(-1, width), in_weight, preferred_element_type=jnp.float32)
    qkv = qkv.astype(jnp.bfloat16).reshape(lon_rows, lat_rows, 3 * width)
    grad_attn = lax.dot_general(
        cotangent.reshape(-1, width),
        out_weight,
        (((1,), (1,)), ((), ())),
        preferred_element_type=jnp.float32,
    )
    grad_attn = grad_attn.astype(jnp.bfloat16).reshape(lon_rows, lat_rows, width)
    query = qkv[..., :width]
    keys = qkv[..., width : 2 * width]
    values = qkv[..., 2 * width :]
    row_query = query[..., :half_width]
    row_grad = grad_attn[..., :half_width]
    query_heads = split_heads(row_query, head_count)
    grad_heads = split_heads(row_grad, head_count)
    keys_all, values_all = (
        lax.all_gather(keys[..., :half_width], "lon", axis=0, tiled=True),
        lax.all_gather(values[..., :half_width], "lon", axis=0, tiled=True),
    )
    row_dq, row_score, row_weights, row_total, row_deltas = attention_grads(
        query_heads,
        split_heads(keys_all, head_count),
        split_heads(values_all, head_count),
        grad_heads,
        temper,
        "sbhe",
    )
    row_count = lon_rows * lax.axis_size("lon")
    score_piece = lax.slice_in_dim(row_score, 0, row_count, axis=3)
    weight_piece = lax.slice_in_dim(row_weights, 0, row_count, axis=3)
    grad_key = (
        jnp.einsum("bhst,sbhe->tbhe", score_piece, query_heads, preferred_element_type=jnp.float32)
        * temper
    )
    grad_value = jnp.einsum(
        "bhst,sbhe->tbhe", weight_piece, grad_heads, preferred_element_type=jnp.float32
    )
    summed = lax.psum_scatter(
        jnp.concatenate(
            [
                grad_key.reshape(row_count, lat_rows, half_width),
                grad_value.reshape(row_count, lat_rows, half_width),
            ],
            axis=-1,
        ).astype(jnp.bfloat16),
        "lon",
        scatter_dimension=0,
        tiled=True,
    ).astype(jnp.float32)
    row_parts = (
        row_dq.reshape(lon_rows, lat_rows, half_width).astype(jnp.bfloat16),
        summed[..., :half_width].astype(jnp.bfloat16),
        summed[..., half_width:].astype(jnp.bfloat16),
    )
    col_query = query[..., half_width:]
    col_grad = grad_attn[..., half_width:]
    moved = (
        lax.all_to_all(col_query, "lat", split_axis=0, concat_axis=1, tiled=True),
        lax.all_to_all(keys[..., half_width:], "lat", split_axis=0, concat_axis=1, tiled=True),
        lax.all_to_all(values[..., half_width:], "lat", split_axis=0, concat_axis=1, tiled=True),
        lax.all_to_all(col_grad, "lat", split_axis=0, concat_axis=1, tiled=True),
    )
    moved_query = split_heads(moved[0], head_count)
    moved_grad = split_heads(moved[3], head_count)
    col_dq, col_score, col_weights, unused_total, unused_deltas = attention_grads(
        moved_query,
        split_heads(moved[1], head_count),
        split_heads(moved[2], head_count),
        moved_grad,
        temper,
        "bshe",
    )
    col_dk = (
        jnp.einsum("bhst,bshe->bthe", col_score, moved_query, preferred_element_type=jnp.float32)
        * temper
    )
    col_dv = jnp.einsum(
        "bhst,bshe->bthe", col_weights, moved_grad, preferred_element_type=jnp.float32
    )
    block_rows = moved[0].shape[0]
    block_lat = moved[0].shape[1]
    col_parts = (
        lax.all_to_all(
            col_dq.reshape(block_rows, block_lat, half_width).astype(jnp.bfloat16),
            "lat",
            split_axis=1,
            concat_axis=0,
            tiled=True,
        ),
        lax.all_to_all(
            col_dk.reshape(block_rows, block_lat, half_width).astype(jnp.bfloat16),
            "lat",
            split_axis=1,
            concat_axis=0,
            tiled=True,
        ),
        lax.all_to_all(
            col_dv.reshape(block_rows, block_lat, half_width).astype(jnp.bfloat16),
            "lat",
            split_axis=1,
            concat_axis=0,
            tiled=True,
        ),
    )
    grad_qkv = jnp.concatenate(
        [row_parts[0], col_parts[0], row_parts[1], col_parts[1], row_parts[2], col_parts[2]],
        axis=-1,
    )
    grad_fields = lax.dot_general(
        grad_qkv.reshape(-1, 3 * width),
        in_weight,
        (((1,), (1,)), ((), ())),
        preferred_element_type=jnp.float32,
    )
    return grad_fields.astype(jnp.bfloat16).reshape(lon_rows, lat_rows, width)


def solution(mesh):
    placed = (P("lon", "lat", None), P(), P(), P("lon", "lat", None))
    return jax.shard_map(
        per_device, mesh=mesh, in_specs=placed, out_specs=P("lon", "lat", None), check_vma=False
    )
```

profile of v0, /device:TPU:1, one launch (start us, length us, event | category | flops | bytes accessed | tf_op | source)
XLA Modules:
  0.0 268.1 jit_solution(6350622350839510454)
XLA Ops:
  13.6 37.0 %all-gather.3.cloned.1.call-done = bf16[1024,4,256]{2,1,0:T(4,128)(2,1)} async-done(((bf16[64,4,256]{2,1,0:T(4,128)(2,1)}), bf16[1024,4,256]{2,1,0:T(4,128)(2,1)}) %all-gather.3.cloned.1.call-update) | async-done | bytes 2097168 | tf_op jit(solution)/shard_map/all_gather | solution.py:74
  50.6 4.3 %copy.68 = bf16[1024,4,256]{0,2,1:T(8,128)(2,1)} copy(bf16[1024,4,256]{2,1,0:T(4,128)(2,1)} %all-gather.3.cloned.1.call-done) | data formatting | bytes 4194304 | tf_op jit(solution)/shard_map/all_gather | solution.py:74
  54.9 5.0 %fusion.33 = (f32[4,4,64]{2,1,0:T(4,128)S(1)}, f32[4,4,64,1024]{3,2,1,0:T(8,128)}) fusion(bf16[64,4,4,64]{0,3,2,1:T(8,128)(2,1)S(1)} %bitcast.104, bf16[1024,4,4,64]{0,3,2,1:T(8,128)(2,1)} %bitcast.98), kind=kOutput, calls=%fused_computation.57 | convolution fusion | flops 137364480 | bytes 6426624 | tf_op jit(solution)/shard_map/sub | solution.py:24
  59.9 2.7 %fusion.6 = bf16[4,4,64,1024]{3,2,1,0:T(8,128)(2,1)S(1)} fusion(f32[4,4,64,1024]{3,2,1,0:T(8,128)} %get-tuple-element.16, f32[4,4,64]{2,1,0:T(4,128)S(1)} %get-tuple-element.15), kind=kLoop, calls=%fused_computation.12 | loop fusion | flops 2097152 | bytes 6295552 | tf_op jit(solution)/shard_map/convert_element_type | solution.py:27
  66.0 23.0 %all-gather.5.cloned.1.call-done = bf16[1024,4,256]{2,1,0:T(4,128)(2,1)} async-done(((bf16[64,4,256]{2,1,0:T(4,128)(2,1)}), bf16[1024,4,256]{2,1,0:T(4,128)(2,1)}) %all-gather.5.cloned.1.call-update) | async-done | bytes 2097168 | tf_op jit(solution)/shard_map/all_gather | solution.py:75
  89.0 4.3 %copy.72 = bf16[1024,4,256]{0,2,1:T(8,128)(2,1)} copy(bf16[1024,4,256]{2,1,0:T(4,128)(2,1)} %all-gather.5.cloned.1.call-done) | data formatting | bytes 4194304 | tf_op jit(solution)/shard_map/all_gather | solution.py:75
  93.4 3.1 %fusion.22 = f32[4,4,64]{2,1,0:T(4,128)S(1)} fusion(f32[4,4,64,64]{2,3,1,0:T(8,128)S(1)} %copy.103, bf16[1024,4,4,64]{0,3,2,1:T(8,128)(2,1)} %bitcast.101, bf16[4,4,64,1024]{3,2,1,0:T(8,128)(2,1)} %copy-done.1), kind=kOutput, calls=%fused_computation.38 | convolution fusion | flops 134478848 | bytes 4460544 | tf_op jit(solution)/shard_map/bhst,tbhe->sbhe/dot_general | solution.py:28
  96.8 2.6 multiply_convert_fusion.1
  101.5 4.2 %copy.91 = bf16[1024,4,256]{2,1,0:T(4,128)(2,1)} copy(bf16[1024,4,256]{0,2,1:T(8,128)(2,1)} %bitcast.100) | data formatting | bytes 4194304 | tf_op jit(solution)/shard_map/reshape | solution.py:99
  105.7 4.3 %copy.90 = bf16[1024,4,256]{2,1,0:T(4,128)(2,1)} copy(bf16[1024,4,256]{0,2,1:T(8,128)(2,1)} %bitcast.103) | data formatting | bytes 4194304 | tf_op jit(solution)/shard_map/reshape | solution.py:98
  110.0 6.1 %pad_maximum_fusion = bf16[1024,4,512]{2,1,0:T(4,128)(2,1)} fusion(bf16[1024,4,256]{2,1,0:T(4,128)(2,1)} %copy.91, bf16[1024,4,256]{2,1,0:T(4,128)(2,1)} %copy.90), kind=kLoop, calls=%fused_computation.2 | loop fusion | flops 8388608 | bytes 8388608 | tf_op jit(solution)/shard_map/concatenate | solution.py:96
  117.0 17.7 %all_to_all.105 = bf16[64,4,256]{2,1,0:T(4,128)(2,1)S(1)} all-to-all(bf16[64,4,256]{2,1,0:T(4,128)(2,1)S(1)} %copy-done.5), channel_id=1, replica_groups=mesh['lon'=16,'lat'=16] {'lat'}, dimensions={0} | all-to-all | bytes 262144 | tf_op jit(solution)/shard_map/all_to_all | solution.py:118
  134.7 12.9 %all_to_all.106 = bf16[64,4,256]{2,1,0:T(4,128)(2,1)S(1)} all-to-all(bf16[64,4,256]{2,1,0:T(4,128)(2,1)S(1)} %get-tuple-element.7), channel_id=1, replica_groups=mesh['lon'=16,'lat'=16] {'lat'}, dimensions={0} | all-to-all | bytes 262144 | tf_op jit(solution)/shard_map/all_to_all | solution.py:115
  147.6 11.9 %all_to_all.107 = bf16[64,4,256]{2,1,0:T(4,128)(2,1)S(1)} all-to-all(bf16[64,4,256]{2,1,0:T(4,128)(2,1)S(1)} %get-tuple-element.8), channel_id=1, replica_groups=mesh['lon'=16,'lat'=16] {'lat'}, dimensions={0} | all-to-all | bytes 262144 | tf_op jit(solution)/shard_map/all_to_all | solution.py:117
  159.6 3.7 %all-to-all-start = ((bf16[64,4,256]{2,1,0:T(4,128)(2,1)}), bf16[64,4,256]{2,1,0:T(4,128)(2,1)S(1)}, u32[]{:S(2)}, u32[]{:S(2)}) async-start(bf16[64,4,256]{2,1,0:T(4,128)(2,1)} %get-tuple-element.9), calls=%async_computation | async-start | bytes 262144 | tf_op jit(solution)/shard_map/all_to_all | solution.py:116
  164.9 7.2 %all-to-all-done = bf16[64,4,256]{2,1,0:T(4,128)(2,1)S(1)} async-done(((bf16[64,4,256]{2,1,0:T(4,128)(2,1)}), bf16[64,4,256]{2,1,0:T(4,128)(2,1)S(1)}, u32[]{:S(2)}, u32[]{:S(2)}) %all-to-all-start) | async-done | bytes 131104 | tf_op jit(solution)/shard_map/all_to_all | solution.py:116
  177.5 3.5 %all-to-all-start.5 = ((bf16[4,64,256]{2,0,1:T(4,128)(2,1)}), bf16[4,64,256]{2,0,1:T(4,128)(2,1)S(1)}, u32[]{:S(2)}, u32[]{:S(2)}) async-start(bf16[4,64,256]{2,0,1:T(4,128)(2,1)} %copy.93), calls=%async_computation.5 | async-start | bytes 262144 | tf_op jit(solution)/shard_map/all_to_all | solution.py:147
  182.1 7.9 %all-to-all-done.5 = bf16[4,64,256]{2,0,1:T(4,128)(2,1)S(1)} async-done(((bf16[4,64,256]{2,0,1:T(4,128)(2,1)}), bf16[4,64,256]{2,0,1:T(4,128)(2,1)S(1)}, u32[]{:S(2)}, u32[]{:S(2)}) %all-to-all-start.5) | async-done | bytes 131104 | tf_op jit(solution)/shard_map/all_to_all | solution.py:147
  190.0 3.5 %all-to-all-start.4 = ((bf16[4,64,256]{2,0,1:T(4,128)(2,1)}), bf16[4,64,256]{2,0,1:T(4,128)(2,1)S(1)}, u32[]{:S(2)}, u32[]{:S(2)}) async-start(bf16[4,64,256]{2,0,1:T(4,128)(2,1)} %copy.86), calls=%async_computation.4 | async-start | bytes 262144 | tf_op jit(solution)/shard_map/all_to_all | solution.py:140
  194.7 7.7 %all-to-all-done.4 = bf16[4,64,256]{2,0,1:T(4,128)(2,1)S(1)} async-done(((bf16[4,64,256]{2,0,1:T(4,128)(2,1)}), bf16[4,64,256]{2,0,1:T(4,128)(2,1)S(1)}, u32[]{:S(2)}, u32[]{:S(2)}) %all-to-all-start.4) | async-done | bytes 131104 | tf_op jit(solution)/shard_map/all_to_all | solution.py:140
  202.4 3.5 %all-to-all-start.6 = ((bf16[4,64,256]{2,0,1:T(4,128)(2,1)}), bf16[4,64,256]{2,0,1:T(4,128)(2,1)S(1)}, u32[]{:S(2)}, u32[]{:S(2)}) async-start(bf16[4,64,256]{2,0,1:T(4,128)(2,1)} %copy.96), calls=%async_computation.6 | async-start | bytes 262144 | tf_op jit(solution)/shard_map/all_to_all | solution.py:154
  207.4 7.5 %all-to-all-done.6 = bf16[4,64,256]{2,0,1:T(4,128)(2,1)S(1)} async-done(((bf16[4,64,256]{2,0,1:T(4,128)(2,1)}), bf16[4,64,256]{2,0,1:T(4,128)(2,1)S(1)}, u32[]{:S(2)}, u32[]{:S(2)}) %all-to-all-start.6) | async-done | bytes 131104 | tf_op jit(solution)/shard_map/all_to_all | solution.py:154
  215.0 2.9 %fusion.14 = bf16[64,4,4,64]{0,3,2,1:T(8,128)(2,1)S(1)} fusion(bf16[1024,4,4,64]{0,3,2,1:T(8,128)(2,1)} %bitcast.99, bf16[4,4,64,1024]{3,2,1,0:T(8,128)(2,1)} %copy-done.3), kind=kOutput, calls=%fused_computation.30 | convolution fusion | flops 134348800 | bytes 4325376 | tf_op jit(solution)/shard_map/bhst,tbhe->sbhe/dot_general | solution.py:39
  218.4 40.5 %all-reduce.3.cloned.1.call-done = bf16[1024,4,512]{2,1,0:T(4,128)(2,1)} async-done(((bf16[1024,4,512]{2,1,0:T(4,128)(2,1)}), bf16[1024,4,512]{2,1,0:T(4,128)(2,1)}) %all-reduce.3.cloned.1.call-update) | async-done | bytes 4194320
  (81 shorter events, 26.8 us)
Async XLA Ops:
  6.5 1.5 copy-start
  6.5 44.1 %all-gather.3.cloned.1.call-start = ((), (), s32[]{:S(2)}) async-start(), calls=%async_computation.7 | async-start | bytes 2228224 | tf_op jit(solution)/shard_map/all_gather | solution.py:74
  8.8 2.8 %copy-start.4 = (bf16[512,512]{1,0:T(8,128)(2,1)S(1)}, bf16[512,512]{1,0:T(8,128)(2,1)}, u32[]{:S(2)}) copy-start(bf16[512,512]{1,0:T(8,128)(2,1)} %param.6) | copy-start | bytes 1572868
  9.8 79.2 %all-gather.5.cloned.1.call-start = ((), (), s32[]{:S(2)}) async-start(), calls=%async_computation.8 | async-start | bytes 2228224 | tf_op jit(solution)/shard_map/all_gather | solution.py:75
  10.5 248.4 %all-reduce.3.cloned.1.call-start = ((), (), s32[]{:S(2)}) async-start(), calls=%async_computation.9 | async-start | bytes 8388608
  62.6 1.3 copy-start.1
  93.4 3.4 %copy-start.2 = (f32[4,4,64,1024]{3,2,1,0:T(8,128)S(1)}, f32[4,4,64,1024]{3,2,1,0:T(8,128)}, u32[]{:S(2)}) copy-start(f32[4,4,64,1024]{3,2,1,0:T(8,128)} %get-tuple-element.16) | copy-start | bytes 12582916
  99.4 2.1 copy-start.3
  116.1 0.9 copy-start.5
  159.6 12.5 %all-to-all-start = ((bf16[64,4,256]{2,1,0:T(4,128)(2,1)}), bf16[64,4,256]{2,1,0:T(4,128)(2,1)S(1)}, u32[]{:S(2)}, u32[]{:S(2)}) async-start(bf16[64,4,256]{2,1,0:T(4,128)(2,1)} %get-tuple-element.9), calls=%async_computation | async-start | bytes 262144 | tf_op jit(solution)/shard_map/all_to_all | solution.py:116
  173.7 2.3 copy-start.6
  177.5 12.5 %all-to-all-start.5 = ((bf16[4,64,256]{2,0,1:T(4,128)(2,1)}), bf16[4,64,256]{2,0,1:T(4,128)(2,1)S(1)}, u32[]{:S(2)}, u32[]{:S(2)}) async-start(bf16[4,64,256]{2,0,1:T(4,128)(2,1)} %copy.93), calls=%async_computation.5 | async-start | bytes 262144 | tf_op jit(solution)/shard_map/all_to_all | solution.py:147
  181.0 24.9 %copy-start.7 = (u32[256]{0:T(256)S(1)}, u32[256]{0:T(256)}, u32[]{:S(2)}) copy-start(u32[256]{0:T(256)} %constant.16) | copy-start | bytes 3076
  190.0 12.4 %all-to-all-start.4 = ((bf16[4,64,256]{2,0,1:T(4,128)(2,1)}), bf16[4,64,256]{2,0,1:T(4,128)(2,1)S(1)}, u32[]{:S(2)}, u32[]{:S(2)}) async-start(bf16[4,64,256]{2,0,1:T(4,128)(2,1)} %copy.86), calls=%async_computation.4 | async-start | bytes 262144 | tf_op jit(solution)/shard_map/all_to_all | solution.py:140
  202.4 12.5 %all-to-all-start.6 = ((bf16[4,64,256]{2,0,1:T(4,128)(2,1)}), bf16[4,64,256]{2,0,1:T(4,128)(2,1)S(1)}, u32[]{:S(2)}, u32[]{:S(2)}) async-start(bf16[4,64,256]{2,0,1:T(4,128)(2,1)} %copy.96), calls=%async_computation.6 | async-start | bytes 262144 | tf_op jit(solution)/shard_map/all_to_all | solution.py:154
Sparse Core Ops, SparseCore 0:
  9.9 40.6 all-gather.2
  52.5 36.5 all-gather.4
  116.2 142.6 all-reduce.2
where the time goes:
time: 270 us; the launch traced here: 268 us
  waiting for transfers between devices  132 us (49%)
  blocking collectives  42.6 us (16%)
  local copies, waits for them, and re-layouts  34.2 us (13%)
  matrix products  22.5 us (8%)
  starting transfers between devices  14.3 us (5%)
  between operations  14.2 us (5%)
  other arithmetic  8.83 us (3%)
    unnamed x4, waiting for transfers between devices  41.2 us
    all_gather x1, waiting for transfers between devices, per_device(): lax.all_gather(keys[..., :half_width], 'lon', axis=0, tiled=True)  37 us
    all_gather x1, waiting for transfers between devices, per_device(): lax.all_gather(values[..., :half_width], 'lon', axis=0, tiled=True)  23 us
    all_to_all x1, blocking collectives, per_device(): lax.all_to_all(col_grad, 'lat', split_axis=0, concat_axis=1, tiled=True)  17.7 us
    all_to_all x1, blocking collectives, per_device(): lax.all_to_all(col_query, 'lat', split_axis=0, concat_axis=1, tiled=True)  12.9 us
    all_to_all x1, blocking collectives, per_device(): lax.all_to_all(values[..., half_width:], 'lat', split_axis=0, concat_axis...  11.9 us
    all_to_all x1, waiting for transfers between devices, per_device(): lax.all_to_all(col_dk.reshape(block_rows, block_lat, half_width).astype(j...  7.89 us
    all_to_all x1, waiting for transfers between devices, per_device(): lax.all_to_all(col_dq.reshape(block_rows, block_lat, half_width).astype(j...  7.74 us
  transfers between devices with their start and end apart: 7, of which 7 were waited for; matrix products, arithmetic and copies ran while one was open for 11% of the time, Pallas kernels for 0%

commit v1 on v0

v1 whole, which is shorter than its diff:
```python
import math

import jax
import jax.numpy as jnp
from jax import lax
from jax.experimental import pallas as pl
from jax.experimental.pallas import tpu as pltpu
from jax.sharding import PartitionSpec as P

MESH = pl.DeviceIdType.MESH
BF = jnp.bfloat16
F32 = jnp.float32
NT = (((1,), (1,)), ((), ()))
NN = (((1,), (0,)), ((), ()))
TEMPER = 0.125
EXP_SCALE = TEMPER * math.log2(math.e)
GROUP = 16


def dot(a, b, dims=NN):
    return lax.dot_general(a, b, dims, preferred_element_type=F32)


def lat_partner(k, lat):
    i = k // 2
    dz = 4 + (1 - 2 * (i % 2)) * ((i + 1) // 2)
    dx = 1 - k % 2
    return ((lat // 8 + dx) % 2) * 8 + (lat % 8 + dz) % 8


def lon_partner(k, lon):
    i = k // 4
    dy = 2 + (1 - 2 * (i % 2)) * ((i + 1) // 2)
    dx = 1 - (k // 2) % 2
    dc = 1 - k % 2
    return ((lon // 4 + dy) % 4) * 4 + (((lon // 2) % 2 + dx) % 2) * 2 + (lon % 2 + dc) % 2


def kernel(
    x_hbm, w_hbm, wo_hbm, c_hbm, out_ref,
    x, w, wo, cot, gcol, perm, wkv,
    skv, sqg, rkv, rqg, kvt, dkv, sendkv, sendq, retkv, retq,
    cx, cg, cq, ck, cv, cgt, cdq, cdk, cdv, cpart, cret,
    in_sem, own_sem, fs, fr, gs, gr, ks, kr, qs, qr, cs, cr, ds_, dr, es, er,
):
    lon = lax.axis_index("lon")
    lat = lax.axis_index("lat")
    my_l = lon // 4
    my_h = lon % 4

    loads = [
        pltpu.make_async_copy(src, dst, in_sem.at[i])
        for i, (src, dst) in enumerate(((x_hbm, x), (c_hbm, cot), (wo_hbm, wo), (w_hbm, w)))
    ]
    for load in loads:
        load.start()

    barrier = pltpu.get_barrier_semaphore()

    @pl.loop(0, GROUP - 1)
    def _(k):
        pl.semaphore_signal(
            barrier, inc=1, device_id=(lon, lat_partner(k, lat)), device_id_type=MESH
        )
        pl.semaphore_signal(
            barrier, inc=1, device_id=(lon_partner(k, lon), lat), device_id_type=MESH
        )

    def to_lat(k, src, dst, ssem, rsem):
        p = lat_partner(k, lat)
        return pltpu.make_async_remote_copy(
            src_ref=src.at[pl.ds(p * 16, 16)],
            dst_ref=dst.at[pl.ds(lat * 16, 16)],
            send_sem=ssem.at[p],
            recv_sem=rsem.at[lat],
            device_id=(lon, p),
            device_id_type=MESH,
        )

    def from_lat(k, src, dst, ssem, rsem):
        p = lat_partner(k, lat)
        return pltpu.make_async_remote_copy(
            src_ref=src.at[pl.ds(p * 16, 16)],
            dst_ref=dst.at[pl.ds(p * 16, 16)],
            send_sem=ssem.at[p],
            recv_sem=rsem.at[p],
            device_id=(lon, p),
            device_id_type=MESH,
        )

    def to_task(k, src, dst, ssem, rsem):
        p = lon_partner(k, lon)
        return pltpu.make_async_remote_copy(
            src_ref=src.at[p % 4, pl.ds((p // 4) * 64, 64)],
            dst_ref=dst.at[pl.ds(lon * 64, 64)],
            send_sem=ssem.at[p],
            recv_sem=rsem.at[lon],
            device_id=(p, lat),
            device_id_type=MESH,
        )

    def from_task(k, src, dst, ssem, rsem):
        p = lon_partner(k, lon)
        return pltpu.make_async_remote_copy(
            src_ref=src.at[p % 4, pl.ds((p // 4) * 64, 64)],
            dst_ref=dst.at[pl.ds(p * 64, 64)],
            send_sem=ssem.at[p],
            recv_sem=rsem.at[p],
            device_id=(p, lat),
            device_id_type=MESH,
        )

    def back_task(k, src, dst, ssem, rsem):
        p = lon_partner(k, lon)
        return pltpu.make_async_remote_copy(
            src_ref=src.at[pl.ds(p * 64, 64)],
            dst_ref=dst.at[my_h, pl.ds(my_l * 64, 64)],
            send_sem=ssem.at[p],
            recv_sem=rsem.at[lon],
            device_id=(p, lat),
            device_id_type=MESH,
        )

    def home_task(k, src, dst, ssem, rsem):
        p = lon_partner(k, lon)
        return pltpu.make_async_remote_copy(
            src_ref=src.at[pl.ds(p * 64, 64)],
            dst_ref=dst.at[p % 4, pl.ds((p // 4) * 64, 64)],
            send_sem=ssem.at[p],
            recv_sem=rsem.at[p],
            device_id=(p, lat),
            device_id_type=MESH,
        )

    def start_all(make, *args):
        @pl.loop(0, GROUP - 1)
        def _(k):
            make(k, *args).start()

    def wait_recv(make, *args):
        @pl.loop(0, GROUP - 1)
        def _(k):
            make(k, *args).wait_recv()

    def wait_send(make, *args):
        @pl.loop(0, GROUP - 1)
        def _(k):
            make(k, *args).wait_send()

    row = lax.broadcasted_iota(jnp.int32, (256, 256), 0)
    col = lax.broadcasted_iota(jnp.int32, (256, 256), 1)
    perm[...] = jnp.where(col == (row % 64) * 4 + row // 64, 1.0, 0.0).astype(BF)

    loads[0].wait()
    pl.semaphore_wait(barrier, 2 * (GROUP - 1))

    start_all(to_lat, x, cx, fs, fr)

    loads[1].wait()
    loads[2].wait()
    g = dot(cot[...], wo[...], NT).astype(BF)
    gcol[...] = g[:, 256:]
    start_all(to_lat, gcol, cg, gs, gr)

    loads[3].wait()
    for h in range(4):
        wkv[:, h * 128 : h * 128 + 64] = w[:, 512 + h * 64 : 576 + h * 64]
        wkv[:, h * 128 + 64 : h * 128 + 128] = w[:, 1024 + h * 64 : 1088 + h * 64]
    xp = dot(perm[...], x[...]).astype(BF)
    kv = dot(xp, wkv[...]).astype(BF)
    for h in range(4):
        skv[h] = kv[:, h * 128 : h * 128 + 128]
    start_all(to_task, skv, rkv, ks, kr)
    gp_row = dot(perm[...], g[:, :256])
    q = dot(xp, w[:, :256])
    for h in range(4):
        sqg[h] = jnp.concatenate(
            [q[:, h * 64 : h * 64 + 64], gp_row[:, h * 64 : h * 64 + 64]], axis=1
        ).astype(BF)
    start_all(to_task, sqg, rqg, qs, qr)

    own = [
        pltpu.make_async_copy(
            skv.at[my_h, pl.ds(my_l * 64, 64)], rkv.at[pl.ds(lon * 64, 64)], own_sem.at[0]
        ),
        pltpu.make_async_copy(
            sqg.at[my_h, pl.ds(my_l * 64, 64)], rqg.at[pl.ds(lon * 64, 64)], own_sem.at[1]
        ),
        pltpu.make_async_copy(
            x.at[pl.ds(lat * 16, 16)], cx.at[pl.ds(lat * 16, 16)], own_sem.at[2]
        ),
        pltpu.make_async_copy(
            gcol.at[pl.ds(lat * 16, 16)], cg.at[pl.ds(lat * 16, 16)], own_sem.at[3]
        ),
    ]
    for copy in own:
        copy.start()

    own[2].wait()
    wait_recv(from_lat, x, cx, fs, fr)
    cxv = cx[...]
    for t in range(2):
        cq[t] = dot(cxv, w[:, 256 + t * 128 : 384 + t * 128]).astype(BF)
        ck[t] = dot(cxv, w[:, 768 + t * 128 : 896 + t * 128]).astype(BF)
        cv[t] = dot(cxv, w[:, 1280 + t * 128 : 1408 + t * 128]).astype(BF)
    own[3].wait()
    wait_recv(from_lat, gcol, cg, gs, gr)
    for t in range(2):
        cgt[t] = cg[:, t * 128 : t * 128 + 128]
    cdq[...] = jnp.zeros_like(cdq)
    cdk[...] = jnp.zeros_like(cdk)
    cdv[...] = jnp.zeros_like(cdv)
    same = (row // 4) % 4 == (col // 4) % 4
    lane = lax.broadcasted_iota(jnp.int32, (256, 128), 1)

    @pl.loop(0, 4)
    def _(h):
        t = h // 2
        mine = lane // 64 == h % 2

        def keep(a):
            return jnp.where(mine, a.astype(F32), 0.0).astype(BF)

        qz = keep(cq[t])
        kz = keep(ck[t])
        gz = keep(cgt[t])
        st = jnp.where(same, dot(ck[t], qz, NT), -1e30)
        gp = dot(cv[t], gz, NT)
        top = jnp.max(st, axis=0, keepdims=True)
        p = jnp.exp2((st - top) * EXP_SCALE)
        inv = 1.0 / jnp.sum(p, axis=0, keepdims=True)
        delta = jnp.sum(p * gp, axis=0, keepdims=True) * inv
        weights = p * inv
        ds = (weights * (gp - delta)).astype(BF)
        cdk[t] += dot(ds, qz)
        cdv[t] += dot(weights.astype(BF), gz)
        cdq[t] += lax.dot_general(ds, kz, (((0,), (0,)), ((), ())), preferred_element_type=F32)

    part = jnp.zeros((256, 512), F32)
    for t in range(2):
        part += dot((cdq[t] * TEMPER).astype(BF), w[:, 256 + t * 128 : 384 + t * 128], NT)
        part += dot((cdk[t] * TEMPER).astype(BF), w[:, 768 + t * 128 : 896 + t * 128], NT)
        part += dot(cdv[t].astype(BF), w[:, 1280 + t * 128 : 1408 + t * 128], NT)
    cpart[...] = part.astype(BF)
    start_all(to_lat, cpart, cret, cs, cr)
    own_part = pltpu.make_async_copy(
        cpart.at[pl.ds(lat * 16, 16)], cret.at[pl.ds(lat * 16, 16)], own_sem.at[2]
    )
    own_part.start()

    own[0].wait()
    wait_recv(from_task, skv, rkv, ks, kr)
    kvt[...] = rkv[...].astype(F32).T.astype(BF)
    own[1].wait()
    wait_recv(from_task, sqg, rqg, qs, qr)
    dkv[...] = jnp.zeros_like(dkv)

    @pl.loop(0, 4)
    def _(c):
        rows = pl.ds(pl.multiple_of(c * 256, 256), 256)
        qg = rqg[rows, :].astype(F32)
        qz = jnp.where(lane < 64, qg, 0.0).astype(BF)
        gz = jnp.where(lane < 64, 0.0, qg).astype(BF)
        st = dot(rkv[...], qz, NT)
        gp = dot(rkv[...], gz, NT)
        top = jnp.max(st, axis=0, keepdims=True)
        p = jnp.exp2((st - top) * EXP_SCALE)
        inv = 1.0 / jnp.sum(p, axis=0, keepdims=True)
        delta = jnp.sum(p * gp, axis=0, keepdims=True) * inv
        weights = p * inv
        ds = (weights * (gp - delta)).astype(BF)
        dkv[...] += dot(ds, qz) + dot(weights.astype(BF), gz)
        dqt = dot(kvt[...], ds)
        sendq[rows, :] = (dqt.T * TEMPER).astype(BF)

    lane_all = lax.broadcasted_iota(jnp.int32, (1024, 128), 1)
    sendkv[...] = (dkv[...] * jnp.where(lane_all < 64, TEMPER, 1.0)).astype(BF)
    start_all(back_task, sendq, retq, ds_, dr)
    start_all(back_task, sendkv, retkv, es, er)
    own_back = [
        pltpu.make_async_copy(
            sendq.at[pl.ds(lon * 64, 64)], retq.at[my_h, pl.ds(my_l * 64, 64)], own_sem.at[0]
        ),
        pltpu.make_async_copy(
            sendkv.at[pl.ds(lon * 64, 64)], retkv.at[my_h, pl.ds(my_l * 64, 64)], own_sem.at[1]
        ),
    ]
    for copy in own_back:
        copy.start()

    own_back[0].wait()
    wait_recv(home_task, sendq, retq, ds_, dr)
    rp = jnp.zeros((256, 512), F32)
    for h in range(4):
        rp += dot(retq[h][:, :64], w[:, h * 64 : h * 64 + 64], NT)
    own_back[1].wait()
    wait_recv(home_task, sendkv, retkv, es, er)
    for h in range(4):
        rp += dot(retkv[h], wkv[:, h * 128 : h * 128 + 128], NT)
    home = lax.dot_general(
        perm[...], rp.astype(BF), (((0,), (0,)), ((), ())), preferred_element_type=F32
    )
    own_part.wait()
    wait_recv(from_lat, cpart, cret, cs, cr)
    out_ref[...] = (home + cret[...].astype(F32)).astype(BF)

    wait_send(to_lat, x, cx, fs, fr)
    wait_send(to_lat, gcol, cg, gs, gr)
    wait_send(to_task, skv, rkv, ks, kr)
    wait_send(to_task, sqg, rqg, qs, qr)
    wait_send(to_lat, cpart, cret, cs, cr)
    wait_send(back_task, sendq, retq, ds_, dr)
    wait_send(back_task, sendkv, retkv, es, er)


def per_device(fields, in_weight, out_weight, cotangent):
    shape = fields.shape

    def vm(*dims, dtype=BF):
        return pltpu.VMEM(dims, dtype)

    out = pl.pallas_call(
        kernel,
        out_shape=jax.ShapeDtypeStruct((256, 512), BF),
        in_specs=[pl.BlockSpec(memory_space=pl.ANY)] * 4,
        out_specs=pl.BlockSpec(memory_space=pltpu.VMEM),
        scratch_shapes=[
            vm(256, 512), vm(512, 1536), vm(512, 512), vm(256, 512),
            vm(256, 256), vm(256, 256), vm(512, 512),
            vm(4, 256, 128), vm(4, 256, 128), vm(1024, 128), vm(1024, 128), vm(128, 1024),
            vm(1024, 128, dtype=F32), vm(1024, 128), vm(1024, 128),
            vm(4, 256, 128), vm(4, 256, 128),
            vm(256, 512), vm(256, 256), vm(2, 256, 128), vm(2, 256, 128), vm(2, 256, 128),
            vm(2, 256, 128),
            vm(2, 256, 128, dtype=F32), vm(2, 256, 128, dtype=F32), vm(2, 256, 128, dtype=F32),
            vm(256, 512), vm(256, 512),
            pltpu.SemaphoreType.DMA((4,)), pltpu.SemaphoreType.DMA((4,)),
        ] + [pltpu.SemaphoreType.DMA((GROUP,))] * 14,
        compiler_params=pltpu.CompilerParams(
            collective_id=0, has_side_effects=True, vmem_limit_bytes=48 * 2**20
        ),
        name="axial_grads",
    )(fields.reshape(256, 512), in_weight, out_weight, cotangent.reshape(256, 512))
    return out.reshape(shape)


def solution(mesh):
    placed = (P("lon", "lat", None), P(), P(), P("lon", "lat", None))
    return jax.shard_map(
        per_device, mesh=mesh, in_specs=placed, out_specs=P("lon", "lat", None), check_vma=False
    )
```

time: 270 us -> 51.1 us (0.19)
  waiting for transfers between devices: 132 us -> 0 us
  Pallas kernels: 0 us -> 45.6 us
  blocking collectives: 42.6 us -> 0 us
  local copies, waits for them, and re-layouts: 34.2 us -> 5.25 us
  matrix products: 22.5 us -> 0 us
  starting transfers between devices: 14.3 us -> 0 us
  between operations: 14.2 us -> 0.02 us
  other arithmetic: 8.83 us -> 0 us
    all_gather x2 -> x0, waiting for transfers between devices: 60 us -> none  [the longest x1 37 us: per_device(): lax.all_gather(keys[..., :half_width], 'lon', axis=0, tiled=True)]
    pallas_call x0 -> x1, Pallas kernels: none -> 45.6 us  [per_device(): pl.pallas_call(kernel, out_shape=jax.ShapeDtypeStruct((256, 512), BF), in...]
    all_to_all x3 -> x0, blocking collectives: 42.6 us -> none  [the longest x1 17.7 us: per_device(): lax.all_to_all(col_grad, 'lat', split_axis=0, concat_axis=1, tiled=True)]
    unnamed x4 -> x0, waiting for transfers between devices: 41.2 us -> none
    all_to_all x4 -> x0, waiting for transfers between devices: 30.3 us -> none  [the longest x1 7.89 us: per_device(): lax.all_to_all(col_dk.reshape(block_rows, block_lat, half_width).astype(j...]
    dot_general x13 -> x0, matrix products: 17 us -> none  [the longest x2 4.57 us: attention_grads(): jnp.einsum('bhst,' + key_layout + '->' + layout, weights_bf, values, pref...]
    all_to_all x4 -> x0, starting transfers between devices: 14.2 us -> none  [the longest x1 3.69 us: per_device(): lax.all_to_all(keys[..., half_width:], 'lat', split_axis=0, concat_axis=1...]
    reshape x18 -> x3, local copies, waits for them, and re-layouts: 14.4 us -> 2.8 us  [the longest x1 1.02 us: per_device(): cotangent.reshape(256, 512)]
  transfers between devices with their start and end apart: 7 -> 0, of which waited for: 7 -> 0; matrix products, arithmetic and copies ran while one was open for 11% -> 0% of each run, Pallas kernels for 0% -> 0%
where the time goes in v1:
time: 51.1 us; the launch traced here: 50.9 us
  Pallas kernels  45.6 us (89%)
  local copies, waits for them, and re-layouts  5.25 us (10%)
    pallas_call x1, Pallas kernels, per_device(): pl.pallas_call(kernel, out_shape=jax.ShapeDtypeStruct((256, 512), BF), in...  45.6 us
    unnamed x4, local copies, waits for them, and re-layouts  2.44 us

profile of v1, /device:TPU:1, one launch (start us, length us, event | category | flops | bytes accessed | tf_op | source)
XLA Modules:
  0.0 50.9 jit_solution(10773427011061516474)
XLA Ops:
  0.0 1.0 %reshape.9.x_hbm = bf16[256,512]{1,0:T(8,128)(2,1)S(1)} reshape(bf16[64,4,512]{2,1,0:T(4,128)(2,1)} %param.4) | data formatting | bytes 524288 | tf_op jit(solution)/shard_map/reshape | solution.py:343
  1.0 1.0 %reshape.10.c_hbm = bf16[256,512]{1,0:T(8,128)(2,1)S(1)} reshape(bf16[64,4,512]{2,1,0:T(4,128)(2,1)} %param.7) | data formatting | bytes 524288 | tf_op jit(solution)/shard_map/reshape | solution.py:343
  2.0 0.0 copy-start
  2.1 1.4 %copy-done = bf16[512,1536]{1,0:T(8,128)(2,1)S(1)} copy-done((bf16[512,1536]{1,0:T(8,128)(2,1)S(1)}, bf16[512,1536]{1,0:T(8,128)(2,1)}, u32[]{:S(2)}) %copy-start) | copy-done | bytes 1572888
  3.5 0.0 copy-start.1
  3.5 1.0 %copy-done.1 = bf16[512,512]{1,0:T(8,128)(2,1)S(1)} copy-done((bf16[512,512]{1,0:T(8,128)(2,1)S(1)}, bf16[512,512]{1,0:T(8,128)(2,1)}, u32[]{:S(2)}) %copy-start.1) | copy-done | bytes 524312
  4.5 45.6 %axial_grads.1 = bf16[256,512]{1,0:T(8,128)(2,1)S(1)} custom-call(bf16[256,512]{1,0:T(8,128)(2,1)S(1)} %reshape.9.x_hbm, bf16[512,1536]{1,0:T(8,128)(2,1)S(1)} %copy-done, bf16[512,512]{1,0:T(8,128)(2,1)S(1)} %copy-done.1, bf16[256,512]{1,0:T(8,128)(2,1)S(1)} %reshape.10.c_hbm), custom_call_target="tpu_custom_call" | custom-call | tf_op jit(solution)/shard_map/axial_grads/pallas_call | solution.py:322
  50.1 0.8 %reshape.11 = bf16[64,4,512]{2,1,0:T(4,128)(2,1)} reshape(bf16[256,512]{1,0:T(8,128)(2,1)S(1)} %axial_grads.1) | data formatting | bytes 524288 | tf_op jit(solution)/shard_map/reshape | solution.py:344
Async XLA Ops:
  2.0 1.4 %copy-start = (bf16[512,1536]{1,0:T(8,128)(2,1)S(1)}, bf16[512,1536]{1,0:T(8,128)(2,1)}, u32[]{:S(2)}) copy-start(bf16[512,1536]{1,0:T(8,128)(2,1)} %w_hbm.1) | copy-start | bytes 4718596
  3.5 1.0 %copy-start.1 = (bf16[512,512]{1,0:T(8,128)(2,1)S(1)}, bf16[512,512]{1,0:T(8,128)(2,1)}, u32[]{:S(2)}) copy-start(bf16[512,512]{1,0:T(8,128)(2,1)} %wo_hbm.1) | copy-start | bytes 1572868

commit v2 on v0

v2 whole, which is shorter than its diff:
```python
import math

import jax
import jax.numpy as jnp
from jax import lax
from jax.experimental import pallas as pl
from jax.experimental.pallas import tpu as pltpu
from jax.sharding import PartitionSpec as P

MESH = pl.DeviceIdType.MESH
BF = jnp.bfloat16
F32 = jnp.float32
NT = (((1,), (1,)), ((), ()))
NN = (((1,), (0,)), ((), ()))
TEMPER = 0.125
EXP_SCALE = TEMPER * math.log2(math.e)
GROUP = 16


def dot(a, b, dims=NN):
    return lax.dot_general(a, b, dims, preferred_element_type=F32)


def kernel(
    x_hbm, w_hbm, wo_hbm, c_hbm, out_ref,
    x, w, wo, cot, gcol, perm, wkv, mask,
    skv, sqg, rkv, rqg, kt, dkv, sendkv, sendq, retkv, retq, ss, gs,
    cx, cg, cpart, cret, css, cgs,
    in_sem, send_sem, recv_sem,
):
    lon = lax.axis_index("lon")
    lat = lax.axis_index("lat")
    my_l = lax.div(lon, 4)
    my_h = lax.rem(lon, 4)

    loads = [
        pltpu.make_async_copy(src, dst, in_sem.at[i])
        for i, (src, dst) in enumerate(((x_hbm, x), (c_hbm, cot), (wo_hbm, wo), (w_hbm, w)))
    ]
    for load in loads:
        load.start()

    x_hi, z = lax.div(lat, 8), lax.rem(lat, 8)
    lat_peers = [
        (x_hi if dx == 0 else 1 - x_hi) * 8 + lax.rem(z + dz, 8)
        for dz in (4, 3, 5, 2, 6, 1, 7, 0)
        for dx in (1, 0)
        if (dz, dx) != (0, 0)
    ]
    y, x_lo, core = lax.div(lon, 4), lax.rem(lax.div(lon, 2), 2), lax.rem(lon, 2)
    lon_peers = [
        lax.rem(y + dy, 4) * 4
        + (x_lo if dx == 0 else 1 - x_lo) * 2
        + (core if dc == 0 else 1 - core)
        for dy in (2, 1, 3, 0)
        for dx in (1, 0)
        for dc in (1, 0)
        if (dy, dx, dc) != (0, 0, 0)
    ]

    barrier = pltpu.get_barrier_semaphore()
    for p in lat_peers:
        pl.semaphore_signal(barrier, inc=1, device_id=(lon, p), device_id_type=MESH)
    for p in lon_peers:
        pl.semaphore_signal(barrier, inc=1, device_id=(p, lat), device_id_type=MESH)

    def task(ref, p, rows):
        return ref.at[lax.rem(p, 4), pl.ds(pl.multiple_of(lax.div(p, 4) * rows, rows), rows)]

    def block(ref, p, rows):
        return ref.at[pl.ds(pl.multiple_of(p * rows, rows), rows)]

    def exchange(i, peers, device, me, src, dst):
        for p in peers:
            pltpu.make_async_remote_copy(
                src_ref=src(p),
                dst_ref=dst(me),
                send_sem=send_sem.at[i],
                recv_sem=recv_sem.at[i],
                device_id=device(p),
                device_id_type=MESH,
            ).start()
        pltpu.make_async_copy(src(me), dst(me), recv_sem.at[i]).start()

    def over_lat(i, src, dst, rows):
        exchange(
            i, lat_peers, lambda p: (lon, p), lat,
            lambda p: block(src, p, rows), lambda p: block(dst, p, rows),
        )

    def to_tasks(i, src, dst):
        exchange(
            i, lon_peers, lambda p: (p, lat), lon,
            lambda p: task(src, p, 64), lambda p: block(dst, p, 64),
        )

    def from_tasks(i, src, dst, rows):
        for p in lon_peers:
            pltpu.make_async_remote_copy(
                src_ref=block(src, p, rows),
                dst_ref=task(dst, lon, rows),
                send_sem=send_sem.at[i],
                recv_sem=recv_sem.at[i],
                device_id=(p, lat),
                device_id_type=MESH,
            ).start()
        pltpu.make_async_copy(block(src, lon, rows), task(dst, lon, rows), recv_sem.at[i]).start()

    def arrived(i, ref):
        pltpu.make_async_copy(ref, ref, recv_sem.at[i]).wait()

    def sent(i, ref):
        pltpu.make_async_copy(ref, ref, send_sem.at[i]).wait()

    row = lax.broadcasted_iota(jnp.int32, (256, 256), 0)
    col = lax.broadcasted_iota(jnp.int32, (256, 256), 1)
    tile, inner = row // 64, row % 64

    def onehot(at):
        return jnp.where(col == at, 1.0, 0.0).astype(BF)

    perm[0] = onehot((inner // 4) * 16 + tile * 4 + inner % 4)
    perm[1] = onehot((inner % 16) * 16 + tile * 4 + inner // 16)
    perm[2] = onehot((row % 64) * 4 + row // 64)
    mask[...] = jnp.where((row // 4) % 4 == (col // 4) % 4, 0.0, -1e30)

    def regroup(ref, which):
        raw = jnp.concatenate([ref[b * 256 : b * 256 + 256, :] for b in range(4)], axis=1)
        return dot(perm[which], raw).astype(BF)

    def natural(ref):
        moved = regroup(ref, 0)
        return jnp.concatenate(
            [
                jnp.concatenate([moved[t * 64 : t * 64 + 64, b * 128 : b * 128 + 128] for t in range(4)], axis=1)
                for b in range(4)
            ],
            axis=0,
        )

    def lat_major(ref):
        moved = regroup(ref, 1)
        return jnp.concatenate(
            [
                jnp.concatenate(
                    [
                        moved[t * 64 + la * 16 : t * 64 + la * 16 + 16, b * 128 : b * 128 + 128]
                        for t in range(4)
                    ],
                    axis=1,
                )
                for la in range(4)
                for b in range(4)
            ],
            axis=0,
        )

    loads[0].wait()
    pl.semaphore_wait(barrier, 2 * (GROUP - 1))

    over_lat(0, x, cx, 64)
    loads[1].wait()
    loads[2].wait()
    g = dot(natural(cot), wo[...], NT).astype(BF)
    gcol[...] = g[:, 256:]
    over_lat(1, gcol, cg, 16)

    xp = lat_major(x)
    loads[3].wait()
    for h in range(4):
        wkv[:, h * 128 : h * 128 + 64] = w[:, 512 + h * 64 : 576 + h * 64]
        wkv[:, h * 128 + 64 : h * 128 + 128] = w[:, 1024 + h * 64 : 1088 + h * 64]
    kv = dot(xp, wkv[...]).astype(BF)
    for h in range(4):
        skv[h] = kv[:, h * 128 : h * 128 + 128]
    to_tasks(2, skv, rkv)
    g_row = dot(perm[2], g[:, :256])
    q = dot(xp, w[:, :256])
    for h in range(4):
        sqg[h] = jnp.concatenate(
            [q[:, h * 64 : h * 64 + 64], g_row[:, h * 64 : h * 64 + 64]], axis=1
        ).astype(BF)
    to_tasks(3, sqg, rqg)

    def fold(a, op):
        out = a[:8]
        for r in range(8, a.shape[0], 8):
            out = op(out, a[r : r + 8])
        return out

    def attend(tiles, key, value, qz, gz, s_ref, g_ref, bias, emit):
        peak = None
        for t in range(tiles):
            s = dot(key(t), qz, NT)
            if bias is not None:
                s = s + bias(t)
            s_ref[t] = s
            top = fold(s, jnp.maximum)
            peak = top if peak is None else jnp.maximum(peak, top)
        peak = jnp.max(peak, axis=0, keepdims=True) * EXP_SCALE
        total = inner_sum = jnp.zeros((8, 256), F32)
        for t in range(tiles):
            p = jnp.exp2(s_ref[t] * EXP_SCALE - peak)
            gp = dot(value(t), gz, NT)
            s_ref[t] = p
            g_ref[t] = gp
            total = total + fold(p, jnp.add)
            inner_sum = inner_sum + fold(p * gp, jnp.add)
        inv = 1.0 / jnp.sum(total, axis=0, keepdims=True)
        delta = jnp.sum(inner_sum, axis=0, keepdims=True) * inv
        for t in range(tiles):
            weights = s_ref[t] * inv
            ds = (weights * (g_ref[t] - delta)).astype(BF)
            emit(t, ds, weights.astype(BF))

    lane = lax.broadcasted_iota(jnp.int32, (256, 128), 1)
    low = lane < 64
    arrived(0, cx)
    cxv = natural(cx)
    cq = dot(cxv, w[:, 256:512])
    ck32 = dot(cxv, w[:, 768:1024]).astype(BF).astype(F32)
    cv = dot(cxv, w[:, 1280:1536]).astype(BF)
    ckt = ck32.T.astype(BF)
    ck = ck32.astype(BF)
    cq = cq.astype(BF).astype(F32)
    arrived(1, cg)
    dqt, dks, dvs = [], [], []
    for h in range(4):
        lanes = slice(h // 2 * 128, h // 2 * 128 + 128)
        mine = low if h % 2 == 0 else jnp.logical_not(low)
        qz = jnp.where(mine, cq[:, lanes], 0.0).astype(BF)
        gz = jnp.where(mine, cg[:, lanes].astype(F32), 0.0).astype(BF)
        acc = {"q": 0.0}
        dk, dv = [], []

        def emit(t, ds, wb, h=h, qz=qz, gz=gz, acc=acc, dk=dk, dv=dv):
            dk.append(dot(ds, qz))
            dv.append(dot(wb, gz))
            acc["q"] += dot(ckt[h * 64 : h * 64 + 64, t * 128 : t * 128 + 128], ds)

        attend(
            2,
            lambda t: ck[t * 128 : t * 128 + 128, lanes],
            lambda t: cv[t * 128 : t * 128 + 128, lanes],
            qz, gz, css.at[h], cgs.at[h],
            lambda t: mask[t * 128 : t * 128 + 128, :],
            emit,
        )
        dqt.append(acc["q"])
        dks.append(jnp.concatenate(dk, axis=0))
        dvs.append(jnp.concatenate(dv, axis=0))
    dq = (jnp.concatenate(dqt, axis=0).T * TEMPER).astype(BF)
    dk = (jnp.concatenate([dks[0] + dks[1], dks[2] + dks[3]], axis=1) * TEMPER).astype(BF)
    dv = jnp.concatenate([dvs[0] + dvs[1], dvs[2] + dvs[3]], axis=1).astype(BF)
    part = dot(dq, w[:, 256:512], NT) + dot(dk, w[:, 768:1024], NT) + dot(dv, w[:, 1280:1536], NT)
    cpart[...] = part.astype(BF)
    over_lat(4, cpart, cret, 16)

    arrived(2, rkv)
    kt[...] = rkv[...].astype(F32).T[:64].astype(BF)
    dkv[...] = jnp.zeros_like(dkv)
    arrived(3, rqg)

    @pl.loop(0, 4)
    def _(c):
        qg = rqg[pl.ds(pl.multiple_of(c * 256, 256), 256), :].astype(F32)
        qz = jnp.where(low, qg, 0.0).astype(BF)
        gz = jnp.where(low, 0.0, qg).astype(BF)
        acc = {"q": 0.0}

        def keys(t):
            return rkv[t * 128 : t * 128 + 128, :]

        def emit(t, ds, wb):
            dkv[t * 128 : t * 128 + 128, :] += dot(ds, qz) + dot(wb, gz)
            acc["q"] += dot(kt[:, t * 128 : t * 128 + 128], ds)

        attend(8, keys, keys, qz, gz, ss, gs, None, emit)
        dq = (acc["q"].T * TEMPER).astype(F32)
        packed = [
            jnp.concatenate([dq[i * 64 : i * 64 + 32], dq[i * 64 + 32 : i * 64 + 64]], axis=1)
            for i in range(4)
        ]
        sendq[pl.ds(pl.multiple_of(c * 128, 128), 128), :] = jnp.concatenate(packed, axis=0).astype(BF)

    from_tasks(5, sendq, retq, 32)
    lane_all = lax.broadcasted_iota(jnp.int32, (1024, 128), 1)
    sendkv[...] = (dkv[...] * jnp.where(lane_all < 64, TEMPER, 1.0)).astype(BF)
    from_tasks(6, sendkv, retkv, 64)

    arrived(5, retq)
    halves = [
        jnp.concatenate([retq[h][:, k * 64 : k * 64 + 64] for h in range(4)], axis=1)
        for k in range(2)
    ]
    dq = jnp.concatenate(
        [halves[k][la * 32 : la * 32 + 32] for la in range(4) for k in range(2)], axis=0
    )
    rp = dot(dq, w[:, :256], NT)
    arrived(6, retkv)
    rp += dot(jnp.concatenate([retkv[h] for h in range(4)], axis=1), wkv[...], NT)
    home = lax.dot_general(
        perm[2], rp.astype(BF), (((0,), (0,)), ((), ())), preferred_element_type=F32
    )
    arrived(4, cret)
    out_ref[...] = (home + cret[...].astype(F32)).astype(BF)

    sent(0, cx.at[pl.ds(0, 960)])
    sent(1, cg.at[pl.ds(0, 240)])
    sent(2, rkv.at[pl.ds(0, 960)])
    sent(3, rqg.at[pl.ds(0, 960)])
    sent(4, cret.at[pl.ds(0, 240)])
    sent(5, sendq.at[pl.ds(0, 480)])
    sent(6, sendkv.at[pl.ds(0, 960)])


def rows_of_tiles(a):
    return a.reshape(64, 4, 4, 128).transpose(0, 2, 1, 3).reshape(1024, 128)


def per_device(fields, in_weight, out_weight, cotangent):
    shape = fields.shape

    def vm(*dims, dtype=BF):
        return pltpu.VMEM(dims, dtype)

    out = pl.pallas_call(
        kernel,
        out_shape=jax.ShapeDtypeStruct((256, 512), BF),
        in_specs=[pl.BlockSpec(memory_space=pl.ANY)] * 4,
        out_specs=pl.BlockSpec(memory_space=pltpu.VMEM),
        scratch_shapes=[
            vm(1024, 128), vm(512, 1536), vm(512, 512), vm(1024, 128),
            vm(256, 256), vm(3, 256, 256), vm(512, 512), vm(256, 256, dtype=F32),
            vm(4, 256, 128), vm(4, 256, 128), vm(1024, 128), vm(1024, 128), vm(64, 1024),
            vm(1024, 128, dtype=F32), vm(1024, 128), vm(512, 128),
            vm(4, 256, 128), vm(4, 128, 128),
            vm(8, 128, 256, dtype=F32), vm(8, 128, 256, dtype=F32),
            vm(1024, 128), vm(256, 256), vm(256, 512), vm(256, 512),
            vm(4, 2, 128, 256, dtype=F32), vm(4, 2, 128, 256, dtype=F32),
            pltpu.SemaphoreType.DMA((4,)),
            pltpu.SemaphoreType.DMA((7,)), pltpu.SemaphoreType.DMA((7,)),
        ],
        compiler_params=pltpu.CompilerParams(
            collective_id=0, has_side_effects=True, vmem_limit_bytes=60 * 2**20
        ),
        name="axial_grads",
    )(rows_of_tiles(fields), in_weight, out_weight, rows_of_tiles(cotangent))
    return out.reshape(shape)


def solution(mesh):
    placed = (P("lon", "lat", None), P(), P(), P("lon", "lat", None))
    return jax.shard_map(
        per_device, mesh=mesh, in_specs=placed, out_specs=P("lon", "lat", None), check_vma=False
    )
```

time: 270 us -> 39.3 us (0.15)
  waiting for transfers between devices: 132 us -> 0 us
  blocking collectives: 42.6 us -> 0 us
  Pallas kernels: 0 us -> 37.4 us
  local copies, waits for them, and re-layouts: 34.2 us -> 1.72 us
  matrix products: 22.5 us -> 0 us
  starting transfers between devices: 14.3 us -> 0 us
  between operations: 14.2 us -> 0.01 us
  other arithmetic: 8.83 us -> 0 us
    all_gather x2 -> x0, waiting for transfers between devices: 60 us -> none  [the longest x1 37 us: per_device(): lax.all_gather(keys[..., :half_width], 'lon', axis=0, tiled=True)]
    all_to_all x3 -> x0, blocking collectives: 42.6 us -> none  [the longest x1 17.7 us: per_device(): lax.all_to_all(col_grad, 'lat', split_axis=0, concat_axis=1, tiled=True)]
    unnamed x4 -> x0, waiting for transfers between devices: 41.2 us -> none
    pallas_call x0 -> x1, Pallas kernels: none -> 37.4 us  [per_device(): pl.pallas_call(kernel, out_shape=jax.ShapeDtypeStruct((256, 512), BF), in...]
    all_to_all x4 -> x0, waiting for transfers between devices: 30.3 us -> none  [the longest x1 7.89 us: per_device(): lax.all_to_all(col_dk.reshape(block_rows, block_lat, half_width).astype(j...]
    dot_general x13 -> x0, matrix products: 17 us -> none  [the longest x2 4.57 us: attention_grads(): jnp.einsum('bhst,' + key_layout + '->' + layout, weights_bf, values, pref...]
    all_to_all x4 -> x0, starting transfers between devices: 14.2 us -> none  [the longest x1 3.69 us: per_device(): lax.all_to_all(keys[..., half_width:], 'lat', split_axis=0, concat_axis=1...]
    reshape x18 -> x1, local copies, waits for them, and re-layouts: 14.4 us -> 1.72 us  [per_device(): return out.reshape(shape)]
  transfers between devices with their start and end apart: 7 -> 0, of which waited for: 7 -> 0; matrix products, arithmetic and copies ran while one was open for 11% -> 0% of each run, Pallas kernels for 0% -> 0%
where the time goes in v2:
time: 39.3 us; the launch traced here: 39.2 us
  Pallas kernels  37.4 us (95%)
  local copies, waits for them, and re-layouts  1.72 us (4%)
    pallas_call x1, Pallas kernels, per_device(): pl.pallas_call(kernel, out_shape=jax.ShapeDtypeStruct((256, 512), BF), in...  37.4 us
    reshape x1, local copies, waits for them, and re-layouts, per_device(): return out.reshape(shape)  1.72 us

profile of v2, /device:TPU:1, one launch (start us, length us, event | category | flops | bytes accessed | tf_op | source)
XLA Modules:
  0.0 39.2 jit_solution(3348455121069468831)
XLA Ops:
  0.0 37.4 %axial_grads.1 = bf16[256,512]{1,0:T(8,128)(2,1)} custom-call(bf16[1024,128]{1,0:T(8,128)(2,1)} %bitcast.10, bf16[512,1536]{1,0:T(8,128)(2,1)} %w_hbm.1, bf16[512,512]{1,0:T(8,128)(2,1)} %wo_hbm.1, bf16[1024,128]{1,0:T(8,128)(2,1)} %bitcast.11), custom_call_target="tpu_custom_call" | custom-call | tf_op jit(solution)/shard_map/axial_grads/pallas_call | solution.py:327
  37.5 1.7 %reshape.19 = bf16[64,4,512]{2,1,0:T(4,128)(2,1)} reshape(bf16[256,512]{1,0:T(8,128)(2,1)} %axial_grads.1) | data formatting | bytes 524288 | tf_op jit(solution)/shard_map/reshape | solution.py:349

commit v3 on v2

--- a/solution.py
+++ b/solution.py
@@ -24,7 +24,7 @@
 def kernel(
     x_hbm, w_hbm, wo_hbm, c_hbm, out_ref,
     x, w, wo, cot, gcol, perm, wkv, mask,
-    skv, sqg, rkv, rqg, kt, dkv, sendkv, sendq, retkv, retq, ss, gs,
+    skv, sqg, rkv, rqg, kt, qgz, sendkv, sendq, retkv, retq, ss, gs,
     cx, cg, cpart, cret, css, cgs,
     in_sem, send_sem, recv_sem,
 ):
@@ -94,8 +94,8 @@
             lambda p: task(src, p, 64), lambda p: block(dst, p, 64),
         )
 
-    def from_tasks(i, src, dst, rows):
-        for p in lon_peers:
+    def from_tasks(i, src, dst, rows, peers):
+        for p in peers:
             pltpu.make_async_remote_copy(
                 src_ref=block(src, p, rows),
                 dst_ref=task(dst, lon, rows),
@@ -104,7 +104,6 @@
                 device_id=(p, lat),
                 device_id_type=MESH,
             ).start()
-        pltpu.make_async_copy(block(src, lon, rows), task(dst, lon, rows), recv_sem.at[i]).start()
 
     def arrived(i, ref):
         pltpu.make_async_copy(ref, ref, recv_sem.at[i]).wait()
@@ -188,30 +187,28 @@
             out = op(out, a[r : r + 8])
         return out
 
-    def attend(tiles, key, value, qz, gz, s_ref, g_ref, bias, emit):
+    def softmax_stats(tiles, key, value, qz, gz, s_ref, g_ref, bias):
+        size = s_ref.shape[0] // tiles
         peak = None
         for t in range(tiles):
             s = dot(key(t), qz, NT)
             if bias is not None:
                 s = s + bias(t)
-            s_ref[t] = s
+            s_ref[t * size : t * size + size] = s
             top = fold(s, jnp.maximum)
             peak = top if peak is None else jnp.maximum(peak, top)
         peak = jnp.max(peak, axis=0, keepdims=True) * EXP_SCALE
         total = inner_sum = jnp.zeros((8, 256), F32)
         for t in range(tiles):
-            p = jnp.exp2(s_ref[t] * EXP_SCALE - peak)
+            at = slice(t * size, t * size + size)
+            p = jnp.exp2(s_ref[at] * EXP_SCALE - peak)
             gp = dot(value(t), gz, NT)
-            s_ref[t] = p
-            g_ref[t] = gp
+            s_ref[at] = p
+            g_ref[at] = gp
             total = total + fold(p, jnp.add)
             inner_sum = inner_sum + fold(p * gp, jnp.add)
         inv = 1.0 / jnp.sum(total, axis=0, keepdims=True)
-        delta = jnp.sum(inner_sum, axis=0, keepdims=True) * inv
-        for t in range(tiles):
-            weights = s_ref[t] * inv
-            ds = (weights * (g_ref[t] - delta)).astype(BF)
-            emit(t, ds, weights.astype(BF))
+        return inv, jnp.sum(inner_sum, axis=0, keepdims=True) * inv
 
     lane = lax.broadcasted_iota(jnp.int32, (256, 128), 1)
     low = lane < 64
@@ -230,25 +227,18 @@
         mine = low if h % 2 == 0 else jnp.logical_not(low)
         qz = jnp.where(mine, cq[:, lanes], 0.0).astype(BF)
         gz = jnp.where(mine, cg[:, lanes].astype(F32), 0.0).astype(BF)
-        acc = {"q": 0.0}
-        dk, dv = [], []
-
-        def emit(t, ds, wb, h=h, qz=qz, gz=gz, acc=acc, dk=dk, dv=dv):
-            dk.append(dot(ds, qz))
-            dv.append(dot(wb, gz))
-            acc["q"] += dot(ckt[h * 64 : h * 64 + 64, t * 128 : t * 128 + 128], ds)
-
-        attend(
+        inv, delta = softmax_stats(
             2,
             lambda t: ck[t * 128 : t * 128 + 128, lanes],
             lambda t: cv[t * 128 : t * 128 + 128, lanes],
             qz, gz, css.at[h], cgs.at[h],
             lambda t: mask[t * 128 : t * 128 + 128, :],
-            emit,
-        )
-        dqt.append(acc["q"])
-        dks.append(jnp.concatenate(dk, axis=0))
-        dvs.append(jnp.concatenate(dv, axis=0))
+        )
+        weights = css[h] * inv
+        ds = (weights * (cgs[h] - delta)).astype(BF)
+        dks.append(dot(ds, qz))
+        dvs.append(dot(weights.astype(BF), gz))
+        dqt.append(dot(ckt[h * 64 : h * 64 + 64], ds))
     dq = (jnp.concatenate(dqt, axis=0).T * TEMPER).astype(BF)
     dk = (jnp.concatenate([dks[0] + dks[1], dks[2] + dks[3]], axis=1) * TEMPER).astype(BF)
     dv = jnp.concatenate([dvs[0] + dvs[1], dvs[2] + dvs[3]], axis=1).astype(BF)
@@ -257,37 +247,50 @@
     over_lat(4, cpart, cret, 16)
 
     arrived(2, rkv)
-    kt[...] = rkv[...].astype(F32).T[:64].astype(BF)
-    dkv[...] = jnp.zeros_like(dkv)
+    keys_t = rkv[...].astype(F32).T[:64].astype(BF)
+    for t in range(4):
+        kt[t] = keys_t[:, t * 256 : t * 256 + 256]
     arrived(3, rqg)
-
-    @pl.loop(0, 4)
-    def _(c):
-        qg = rqg[pl.ds(pl.multiple_of(c * 256, 256), 256), :].astype(F32)
-        qz = jnp.where(low, qg, 0.0).astype(BF)
-        gz = jnp.where(low, 0.0, qg).astype(BF)
-        acc = {"q": 0.0}
+    stats = []
+    for c in range(4):
+        qg = rqg[c * 256 : c * 256 + 256, :].astype(F32)
+        qgz[c, :256] = jnp.where(low, qg, 0.0).astype(BF)
+        qgz[c, 256:] = jnp.where(low, 0.0, qg).astype(BF)
 
         def keys(t):
             return rkv[t * 128 : t * 128 + 128, :]
 
-        def emit(t, ds, wb):
-            dkv[t * 128 : t * 128 + 128, :] += dot(ds, qz) + dot(wb, gz)
-            acc["q"] += dot(kt[:, t * 128 : t * 128 + 128], ds)
-
-        attend(8, keys, keys, qz, gz, ss, gs, None, emit)
-        dq = (acc["q"].T * TEMPER).astype(F32)
+        stats.append(
+            softmax_stats(8, keys, keys, qgz[c, :256], qgz[c, 256:], ss.at[c], gs.at[c], None)
+        )
+
+    dqt = [jnp.zeros((64, 256), F32) for _ in range(4)]
+    half_scale = jnp.where(low, TEMPER, 1.0)
+    for dy in (2, 1, 3, 0):
+        at = lax.rem(y + dy, 4)
+        rows = pl.ds(pl.multiple_of(at * 256, 256), 256)
+        acc = jnp.zeros((256, 128), F32)
+        for c in range(4):
+            inv, delta = stats[c]
+            weights = ss[c, rows] * inv
+            ds = (weights * (gs[c, rows] - delta)).astype(BF)
+            acc += dot(ds, qgz[c, :256]) + dot(weights.astype(BF), qgz[c, 256:])
+            dqt[c] += dot(kt[at], ds)
+        sendkv[rows, :] = (acc * half_scale).astype(BF)
+        from_tasks(6, sendkv, retkv, 64, lon_peers[4 * ((2, 1, 3, 0).index(dy)) :][:4])
+    pltpu.make_async_copy(block(sendkv, lon, 64), task(retkv, lon, 64), recv_sem.at[6]).start()
+    for c in range(4):
+        dq = dqt[c].T * TEMPER
         packed = [
             jnp.concatenate([dq[i * 64 : i * 64 + 32], dq[i * 64 + 32 : i * 64 + 64]], axis=1)
             for i in range(4)
         ]
-        sendq[pl.ds(pl.multiple_of(c * 128, 128), 128), :] = jnp.concatenate(packed, axis=0).astype(BF)
-
-    from_tasks(5, sendq, retq, 32)
-    lane_all = lax.broadcasted_iota(jnp.int32, (1024, 128), 1)
-    sendkv[...] = (dkv[...] * jnp.where(lane_all < 64, TEMPER, 1.0)).astype(BF)
-    from_tasks(6, sendkv, retkv, 64)
-
+        sendq[c * 128 : c * 128 + 128, :] = jnp.concatenate(packed, axis=0).astype(BF)
+    from_tasks(5, sendq, retq, 32, lon_peers)
+    pltpu.make_async_copy(block(sendq, lon, 32), task(retq, lon, 32), recv_sem.at[5]).start()
+
+    arrived(6, retkv)
+    rp = dot(jnp.concatenate([retkv[h] for h in range(4)], axis=1), wkv[...], NT)
     arrived(5, retq)
     halves = [
         jnp.concatenate([retq[h][:, k * 64 : k * 64 + 64] for h in range(4)], axis=1)
@@ -296,9 +299,7 @@
     dq = jnp.concatenate(
         [halves[k][la * 32 : la * 32 + 32] for la in range(4) for k in range(2)], axis=0
     )
-    rp = dot(dq, w[:, :256], NT)
-    arrived(6, retkv)
-    rp += dot(jnp.concatenate([retkv[h] for h in range(4)], axis=1), wkv[...], NT)
+    rp += dot(dq, w[:, :256], NT)
     home = lax.dot_general(
         perm[2], rp.astype(BF), (((0,), (0,)), ((), ())), preferred_element_type=F32
     )
@@ -332,20 +333,23 @@
         scratch_shapes=[
             vm(1024, 128), vm(512, 1536), vm(512, 512), vm(1024, 128),
             vm(256, 256), vm(3, 256, 256), vm(512, 512), vm(256, 256, dtype=F32),
-            vm(4, 256, 128), vm(4, 256, 128), vm(1024, 128), vm(1024, 128), vm(64, 1024),
-            vm(1024, 128, dtype=F32), vm(1024, 128), vm(512, 128),
+            vm(4, 256, 128), vm(4, 256, 128), vm(1024, 128), vm(1024, 128), vm(4, 64, 256),
+            vm(4, 512, 128), vm(1024, 128), vm(512, 128),
             vm(4, 256, 128), vm(4, 128, 128),
-            vm(8, 128, 256, dtype=F32), vm(8, 128, 256, dtype=F32),
+            vm(4, 1024, 256, dtype=F32), vm(4, 1024, 256, dtype=F32),
             vm(1024, 128), vm(256, 256), vm(256, 512), vm(256, 512),
-            vm(4, 2, 128, 256, dtype=F32), vm(4, 2, 128, 256, dtype=F32),
+            vm(4, 256, 256, dtype=F32), vm(4, 256, 256, dtype=F32),
             pltpu.SemaphoreType.DMA((4,)),
             pltpu.SemaphoreType.DMA((7,)), pltpu.SemaphoreType.DMA((7,)),
         ],
         compiler_params=pltpu.CompilerParams(
-            collective_id=0, has_side_effects=True, vmem_limit_bytes=60 * 2**20
+            collective_id=0, has_side_effects=True, vmem_limit_bytes=40 * 2**20
         ),
         name="axial_grads",
-    )(rows_of_tiles(fields), in_weight, out_weight, rows_of_tiles(cotangent))
+    )(*(
+        pltpu.with_memory_space_constraint(a, pltpu.HBM)
+        for a in (rows_of_tiles(fields), in_weight, out_weight, rows_of_tiles(cotangent))
+    ))
     return out.reshape(shape)
 
 

time: 39.3 us -> 36.6 us (0.931)
  Pallas kernels: 37.4 us -> 35.8 us
  local copies, waits for them, and re-layouts: 1.72 us -> 0.77 us
    pallas_call x1, Pallas kernels: 37.4 us -> 35.8 us  [per_device(): pl.pallas_call(kernel, out_shape=jax.ShapeDtypeStruct((256, 512), BF), in...]
    reshape x1, local copies, waits for them, and re-layouts: 1.72 us -> 0.77 us  [per_device(): return out.reshape(shape)]
where the time goes in v3:
time: 36.6 us; the launch traced here: 36.5 us
  Pallas kernels  35.8 us (98%)
  local copies, waits for them, and re-layouts  0.77 us (2%)
    pallas_call x1, Pallas kernels, per_device(): pl.pallas_call(kernel, out_shape=jax.ShapeDtypeStruct((256, 512), BF), in...  35.8 us
    reshape x1, local copies, waits for them, and re-layouts, per_device(): return out.reshape(shape)  0.77 us

profile of v3, /device:TPU:1, one launch (start us, length us, event | category | flops | bytes accessed | tf_op | source)
XLA Modules:
  0.0 36.5 jit_solution(8484959481837019704)
XLA Ops:
  0.0 35.8 %axial_grads.1 = bf16[256,512]{1,0:T(8,128)(2,1)S(1)} custom-call(bf16[1024,128]{1,0:T(8,128)(2,1)} %bitcast.10, bf16[512,1536]{1,0:T(8,128)(2,1)} %w_hbm.1, bf16[512,512]{1,0:T(8,128)(2,1)} %wo_hbm.1, bf16[1024,128]{1,0:T(8,128)(2,1)} %bitcast.11), custom_call_target="tpu_custom_call" | custom-call | tf_op jit(solution)/shard_map/axial_grads/pallas_call | solution.py:328
  35.8 0.8 %reshape.19 = bf16[64,4,512]{2,1,0:T(4,128)(2,1)} reshape(bf16[256,512]{1,0:T(8,128)(2,1)S(1)} %axial_grads.1) | data formatting | bytes 524288 | tf_op jit(solution)/shard_map/reshape | solution.py:353

commit v4 on v3

v4 whole, which is shorter than its diff:
```python
import math

import jax
import jax.numpy as jnp
from jax import lax
from jax.experimental import pallas as pl
from jax.experimental.pallas import tpu as pltpu
from jax.sharding import PartitionSpec as P

MESH = pl.DeviceIdType.MESH
BF = jnp.bfloat16
F32 = jnp.float32
NT = (((1,), (1,)), ((), ()))
NN = (((1,), (0,)), ((), ()))
TEMPER = 0.125
EXP_SCALE = TEMPER * math.log2(math.e)
GROUP = 16


def dot(a, b, dims=NN):
    return lax.dot_general(a, b, dims, preferred_element_type=F32)


def kernel(
    x_hbm, w_hbm, wo_hbm, c_hbm, out_ref,
    x, w, wo, cot, perm, wkv, mask,
    skv, sqg, rkv, rqg, kt, qgz, sendkv, sendq, retkv, retq, ss, gs,
    xg, cxg, cpart, cret, css, cgs,
    in_sem, send_sem, recv_sem, chunk_sem,
):
    lon = lax.axis_index("lon")
    lat = lax.axis_index("lat")
    my_l = lax.div(lon, 4)
    my_h = lax.rem(lon, 4)

    loads = [
        pltpu.make_async_copy(src, dst, in_sem.at[i])
        for i, (src, dst) in enumerate(((x_hbm, x), (c_hbm, cot), (wo_hbm, wo), (w_hbm, w)))
    ]
    for load in loads:
        load.start()

    z_lat = lax.rem(lat, 8)
    lat_peers = [
        x_hi * 8 + lax.rem(z_lat + dz, 8) for dz in (4, 3, 5, 2, 6, 1, 7, 0) for x_hi in (0, 1)
    ]
    y, x_lo, core = lax.div(lon, 4), lax.rem(lax.div(lon, 2), 2), lax.rem(lon, 2)
    beside = y * 4 + (1 - x_lo) * 2 + core
    lon_peers = [
        lax.rem(y + dy, 4) * 4
        + (x_lo if dx == 0 else 1 - x_lo) * 2
        + (core if dc == 0 else 1 - core)
        for dy in (2, 1, 3, 0)
        for dx in (1, 0)
        for dc in (1, 0)
        if (dy, dx, dc) != (0, 0, 0)
    ]

    barrier = pltpu.get_barrier_semaphore()
    for p in lat_peers:
        pl.semaphore_signal(barrier, inc=1, device_id=(beside, p), device_id_type=MESH)
    for p in lon_peers:
        pl.semaphore_signal(barrier, inc=1, device_id=(p, lat), device_id_type=MESH)

    def task(ref, p, rows):
        return ref.at[lax.rem(p, 4), pl.ds(pl.multiple_of(lax.div(p, 4) * rows, rows), rows)]

    def block(ref, p, rows):
        return ref.at[pl.ds(pl.multiple_of(p * rows, rows), rows)]

    def over_lat(i, src, dst, rows):
        for p in lat_peers:
            pltpu.make_async_remote_copy(
                src_ref=block(src, p, rows),
                dst_ref=block(dst, lat, rows),
                send_sem=send_sem.at[i],
                recv_sem=recv_sem.at[i],
                device_id=(beside, p),
                device_id_type=MESH,
            ).start()

    def to_tasks(i, src, dst, landed):
        for p in lon_peers:
            pltpu.make_async_remote_copy(
                src_ref=task(src, p, 64),
                dst_ref=block(dst, lon, 64),
                send_sem=send_sem.at[i],
                recv_sem=landed,
                device_id=(p, lat),
                device_id_type=MESH,
            ).start()
        pltpu.make_async_copy(task(src, lon, 64), block(dst, lon, 64), landed).start()

    def from_tasks(i, src, dst, rows, peers):
        for p in peers:
            pltpu.make_async_remote_copy(
                src_ref=block(src, p, rows),
                dst_ref=task(dst, lon, rows),
                send_sem=send_sem.at[i],
                recv_sem=recv_sem.at[i],
                device_id=(p, lat),
                device_id_type=MESH,
            ).start()

    def arrived(i, ref):
        pltpu.make_async_copy(ref, ref, recv_sem.at[i]).wait()

    def sent(i, ref):
        pltpu.make_async_copy(ref, ref, send_sem.at[i]).wait()

    row = lax.broadcasted_iota(jnp.int32, (256, 256), 0)
    col = lax.broadcasted_iota(jnp.int32, (256, 256), 1)
    tile, inner = row // 64, row % 64

    def onehot(at):
        return jnp.where(col == at, 1.0, 0.0).astype(BF)

    perm[0] = onehot((inner // 4) * 16 + tile * 4 + inner % 4)
    perm[1] = onehot((inner % 16) * 16 + tile * 4 + inner // 16)
    perm[2] = onehot((row % 64) * 4 + row // 64)
    row = lax.broadcasted_iota(jnp.int32, (128, 512), 0)
    col = lax.broadcasted_iota(jnp.int32, (128, 512), 1)
    mask[...] = jnp.where((row // 4) % 2 == (col // 4) % 2, 0.0, -1e30)

    def regroup(blocks, which):
        return dot(perm[which], jnp.concatenate(blocks, axis=1)).astype(BF)

    def natural(blocks):
        moved = regroup(blocks, 0)
        return jnp.concatenate(
            [
                jnp.concatenate(
                    [moved[t * 64 : t * 64 + 64, b * 128 : b * 128 + 128] for t in range(4)], axis=1
                )
                for b in range(len(blocks))
            ],
            axis=0,
        )

    def quarters(ref):
        return [ref[b * 256 : b * 256 + 256, :] for b in range(4)]

    def lat_major(blocks):
        moved = regroup(blocks, 1)
        return jnp.concatenate(
            [
                jnp.concatenate(
                    [
                        moved[t * 64 + la * 16 : t * 64 + la * 16 + 16, b * 128 : b * 128 + 128]
                        for t in range(4)
                    ],
                    axis=1,
                )
                for la in range(4)
                for b in range(4)
            ],
            axis=0,
        )

    loads[1].wait()
    loads[2].wait()
    g = dot(natural(quarters(cot)), wo[...], NT)
    loads[0].wait()
    for half in range(2):
        for p in range(GROUP):
            xg[half, p * 48 : p * 48 + 32, :] = x[p * 64 + half * 32 : p * 64 + half * 32 + 32, :]
            xg[half, p * 48 + 32 : p * 48 + 48, :] = jnp.concatenate(
                [
                    g[p * 16 + half * 8 : p * 16 + half * 8 + 8, 256 + t * 128 : 384 + t * 128]
                    for t in range(2)
                ],
                axis=0,
            ).astype(BF)

    def front_row():
        xp = lat_major(quarters(x))
        loads[3].wait()
        for h in range(4):
            wkv[:, h * 128 : h * 128 + 64] = w[:, 512 + h * 64 : 576 + h * 64]
            wkv[:, h * 128 + 64 : h * 128 + 128] = w[:, 1024 + h * 64 : 1088 + h * 64]
        kv = dot(xp, wkv[...]).astype(BF)
        g_row = dot(perm[2], g[:, :256].astype(BF))
        q = dot(xp, w[:, :256])
        for h in range(4):
            skv[h] = kv[:, h * 128 : h * 128 + 128]
            sqg[h] = jnp.concatenate(
                [q[:, h * 64 : h * 64 + 64], g_row[:, h * 64 : h * 64 + 64]], axis=1
            ).astype(BF)

    front_row()
    pl.semaphore_wait(barrier, 2 * GROUP - 1)
    to_tasks(2, skv, rkv, recv_sem.at[2])
    to_tasks(3, sqg, rqg, chunk_sem.at[y])
    over_lat(0, xg.at[0], cxg.at[0], 48)
    over_lat(1, xg.at[1], cxg.at[1], 48)
    def fold(a, op):
        out = a[:8]
        for r in range(8, a.shape[0], 8):
            out = op(out, a[r : r + 8])
        return out

    def softmax_stats(tiles, key, value, qz, gz, s_ref, g_ref, bias):
        size = s_ref.shape[0] // tiles
        peak = None
        for t in range(tiles):
            s = dot(key(t), qz, NT)
            if bias is not None:
                s = s + bias(t)
            s_ref[t * size : t * size + size] = s
            top = fold(s, jnp.maximum)
            peak = top if peak is None else jnp.maximum(peak, top)
        peak = jnp.max(peak, axis=0, keepdims=True) * EXP_SCALE
        total = inner_sum = jnp.zeros((8, qz.shape[0]), F32)
        for t in range(tiles):
            at = slice(t * size, t * size + size)
            p = jnp.exp2(s_ref[at] * EXP_SCALE - peak)
            gp = dot(value(t), gz, NT)
            s_ref[at] = p
            g_ref[at] = gp
            total = total + fold(p, jnp.add)
            inner_sum = inner_sum + fold(p * gp, jnp.add)
        inv = 1.0 / jnp.sum(total, axis=0, keepdims=True)
        return inv, jnp.sum(inner_sum, axis=0, keepdims=True) * inv

    low = lax.broadcasted_iota(jnp.int32, (256, 128), 1) < 64
    head_of_lane = lax.broadcasted_iota(jnp.int32, (128, 256), 1) // 64

    def columns(half, i_in, i_out):
        arrived(i_in, cxg.at[half])
        got = cxg.at[half]
        tokens = natural(
            [
                jnp.concatenate(
                    [got[p * 48 : p * 48 + 32, :] for p in range(b * 8, b * 8 + 8)], axis=0
                )
                for b in range(2)
            ]
        )
        grads = [got[p * 48 + 32 : p * 48 + 48, :].astype(F32) for p in range(GROUP)]
        grads = jnp.concatenate(
            [
                jnp.concatenate([a[t * 8 : t * 8 + 8] for a in grads], axis=0) for t in range(2)
            ],
            axis=1,
        )
        q = dot(tokens, w[:, 256:512]).astype(BF).astype(F32)
        k = dot(tokens, w[:, 768:1024]).astype(BF)
        v = dot(tokens, w[:, 1280:1536]).astype(BF)
        k_t = k.astype(F32).T.astype(BF)

        def by_head(a):
            return jnp.concatenate(
                [jnp.where(head_of_lane == h, a, 0.0).astype(BF) for h in range(4)], axis=0
            )

        qz, gz = by_head(q), by_head(grads)
        s_ref, g_ref = css.at[half], cgs.at[half]
        inv, delta = softmax_stats(
            1, lambda t: k, lambda t: v, qz, gz, s_ref, g_ref, lambda t: mask[...]
        )
        weights = s_ref[...] * inv
        ds = (weights * (g_ref[...] - delta)).astype(BF)
        dk = (dot(ds, qz) * TEMPER).astype(BF)
        dv = dot(weights.astype(BF), gz).astype(BF)
        dq_t = jnp.concatenate(
            [dot(k_t[h * 64 : h * 64 + 64], ds[:, h * 128 : h * 128 + 128]) for h in range(4)],
            axis=0,
        )
        dq = (dq_t.T * TEMPER).astype(BF)
        part = (
            dot(dq, w[:, 256:512], NT) + dot(dk, w[:, 768:1024], NT) + dot(dv, w[:, 1280:1536], NT)
        )
        for p in range(GROUP):
            cpart[half, p * 32 : p * 32 + 32, :] = jnp.concatenate(
                [part[p * 8 : p * 8 + 8, t * 128 : t * 128 + 128] for t in range(4)], axis=0
            ).astype(BF)
        over_lat(i_out, cpart.at[half], cret.at[half], 32)

    def chunk_rows(dy, size):
        return pl.ds(pl.multiple_of(lax.rem(y + dy, 4) * size, size), size)

    def row_stats():
        arrived(2, rkv)
        keys_t = rkv[...].astype(F32).T[:64].astype(BF)
        for t in range(4):
            kt[t] = keys_t[:, t * 256 : t * 256 + 256]
        stats = []
        for c, dy in enumerate((0, 1, 3, 2)):
            rows = rqg.at[chunk_rows(dy, 256)]
            pltpu.make_async_copy(rows, rows, chunk_sem.at[lax.rem(y + dy, 4)]).wait()
            qg = rows[...].astype(F32)
            qgz[c, :256] = jnp.where(low, qg, 0.0).astype(BF)
            qgz[c, 256:] = jnp.where(low, 0.0, qg).astype(BF)

            def keys(t):
                return rkv[t * 128 : t * 128 + 128, :]

            stats.append(
                softmax_stats(8, keys, keys, qgz[c, :256], qgz[c, 256:], ss.at[c], gs.at[c], None)
            )
        return stats

    def row_grads(stats):
        dqt = [jnp.zeros((64, 256), F32) for _ in range(4)]
        half_scale = jnp.where(low, TEMPER, 1.0)
        for dy in (2, 1, 3, 0):
            at = lax.rem(y + dy, 4)
            rows = pl.ds(pl.multiple_of(at * 256, 256), 256)
            acc = jnp.zeros((256, 128), F32)
            for c in range(4):
                inv, delta = stats[c]
                weights = ss[c, rows] * inv
                ds = (weights * (gs[c, rows] - delta)).astype(BF)
                acc += dot(ds, qgz[c, :256]) + dot(weights.astype(BF), qgz[c, 256:])
                dqt[c] += dot(kt[at], ds)
            sendkv[rows, :] = (acc * half_scale).astype(BF)
            from_tasks(6, sendkv, retkv, 64, lon_peers[4 * ((2, 1, 3, 0).index(dy)) :][:4])
        pltpu.make_async_copy(block(sendkv, lon, 64), task(retkv, lon, 64), recv_sem.at[6]).start()
        for c, dy in ((3, 2), (1, 1), (2, 3), (0, 0)):
            dq = dqt[c].T * TEMPER
            packed = [
                jnp.concatenate([dq[i * 64 : i * 64 + 32], dq[i * 64 + 32 : i * 64 + 64]], axis=1)
                for i in range(4)
            ]
            sendq[chunk_rows(dy, 128), :] = jnp.concatenate(packed, axis=0).astype(BF)
            from_tasks(5, sendq, retq, 32, lon_peers[4 * ((2, 1, 3, 0).index(dy)) :][:4])
        pltpu.make_async_copy(block(sendq, lon, 32), task(retq, lon, 32), recv_sem.at[5]).start()

    columns(0, 0, 4)
    stats = row_stats()
    row_grads(stats)
    columns(1, 1, 7)

    def home(a):
        return lax.dot_general(
            perm[2], a, (((0,), (0,)), ((), ())), preferred_element_type=F32
        ).astype(BF)

    arrived(4, cret.at[0])
    arrived(7, cret.at[1])
    back = [cret[half].astype(F32) for half in range(2)]
    total = jnp.concatenate(
        [
            jnp.concatenate(
                [
                    back[half][p * 32 + t * 8 : p * 32 + t * 8 + 8]
                    for p in range(GROUP)
                    for half in range(2)
                ],
                axis=0,
            )
            for t in range(4)
        ],
        axis=1,
    )
    arrived(6, retkv)
    total += dot(home(jnp.concatenate([retkv[h] for h in range(4)], axis=1)), wkv[...], NT)
    arrived(5, retq)
    halves = [
        jnp.concatenate([retq[h][:, k * 64 : k * 64 + 64] for h in range(4)], axis=1)
        for k in range(2)
    ]
    dq = jnp.concatenate(
        [halves[k][la * 32 : la * 32 + 32] for la in range(4) for k in range(2)], axis=0
    )
    out_ref[...] = (total + dot(home(dq), w[:, :256], NT)).astype(BF)

    sent(0, cxg.at[0])
    sent(1, cxg.at[1])
    sent(2, rkv.at[pl.ds(0, 960)])
    sent(3, rqg.at[pl.ds(0, 960)])
    sent(4, cret.at[0])
    sent(7, cret.at[1])
    sent(5, sendq.at[pl.ds(0, 480)])
    sent(6, sendkv.at[pl.ds(0, 960)])


def rows_of_tiles(a):
    return a.reshape(64, 4, 4, 128).transpose(0, 2, 1, 3).reshape(1024, 128)


def per_device(fields, in_weight, out_weight, cotangent):
    shape = fields.shape

    def vm(*dims, dtype=BF):
        return pltpu.VMEM(dims, dtype)

    out = pl.pallas_call(
        kernel,
        out_shape=jax.ShapeDtypeStruct((256, 512), BF),
        in_specs=[pl.BlockSpec(memory_space=pl.ANY)] * 4,
        out_specs=pl.BlockSpec(memory_space=pltpu.VMEM),
        scratch_shapes=[
            vm(1024, 128), vm(512, 1536), vm(512, 512), vm(1024, 128),
            vm(3, 256, 256), vm(512, 512), vm(128, 512, dtype=F32),
            vm(4, 256, 128), vm(4, 256, 128), vm(1024, 128), vm(1024, 128), vm(4, 64, 256),
            vm(4, 512, 128), vm(1024, 128), vm(512, 128),
            vm(4, 256, 128), vm(4, 128, 128),
            vm(4, 1024, 256, dtype=F32), vm(4, 1024, 256, dtype=F32),
            vm(2, 768, 128), vm(2, 768, 128), vm(2, 512, 128), vm(2, 512, 128),
            vm(2, 128, 512, dtype=F32), vm(2, 128, 512, dtype=F32),
            pltpu.SemaphoreType.DMA((4,)),
            pltpu.SemaphoreType.DMA((8,)), pltpu.SemaphoreType.DMA((8,)),
            pltpu.SemaphoreType.DMA((4,)),
        ],
        compiler_params=pltpu.CompilerParams(
            collective_id=0, has_side_effects=True, vmem_limit_bytes=40 * 2**20
        ),
        name="axial_grads",
    )(*(
        pltpu.with_memory_space_constraint(a, pltpu.HBM)
        for a in (rows_of_tiles(fields), in_weight, out_weight, rows_of_tiles(cotangent))
    ))
    return out.reshape(shape)


def solution(mesh):
    placed = (P("lon", "lat", None), P(), P(), P("lon", "lat", None))
    return jax.shard_map(
        per_device, mesh=mesh, in_specs=placed, out_specs=P("lon", "lat", None), check_vma=False
    )
```

time: 36.6 us -> 35.3 us (0.964)
  Pallas kernels: 35.8 us -> 34.4 us
    pallas_call x1, Pallas kernels: 35.8 us -> 34.4 us  [per_device(): pl.pallas_call(kernel, out_shape=jax.ShapeDtypeStruct((256, 512), BF), in...]
where the time goes in v4:
time: 35.3 us; the launch traced here: 35.2 us
  Pallas kernels  34.4 us (97%)
  local copies, waits for them, and re-layouts  0.77 us (2%)
    pallas_call x1, Pallas kernels, per_device(): pl.pallas_call(kernel, out_shape=jax.ShapeDtypeStruct((256, 512), BF), in...  34.4 us
    reshape x1, local copies, waits for them, and re-layouts, per_device(): return out.reshape(shape)  0.77 us

profile of v4, /device:TPU:1, one launch (start us, length us, event | category | flops | bytes accessed | tf_op | source)
XLA Modules:
  0.0 35.2 jit_solution(17763328492930861617)
XLA Ops:
  0.0 34.4 %axial_grads.1 = bf16[256,512]{1,0:T(8,128)(2,1)S(1)} custom-call(bf16[1024,128]{1,0:T(8,128)(2,1)} %bitcast.10, bf16[512,1536]{1,0:T(8,128)(2,1)} %w_hbm.1, bf16[512,512]{1,0:T(8,128)(2,1)} %wo_hbm.1, bf16[1024,128]{1,0:T(8,128)(2,1)} %bitcast.11), custom_call_target="tpu_custom_call" | custom-call | tf_op jit(solution)/shard_map/axial_grads/pallas_call | solution.py:388
  34.4 0.8 %reshape.19 = bf16[64,4,512]{2,1,0:T(4,128)(2,1)} reshape(bf16[256,512]{1,0:T(8,128)(2,1)S(1)} %axial_grads.1) | data formatting | bytes 524288 | tf_op jit(solution)/shard_map/reshape | solution.py:414

commit v5 on v4

--- a/solution.py
+++ b/solution.py
@@ -26,7 +26,7 @@
     x, w, wo, cot, perm, wkv, mask,
     skv, sqg, rkv, rqg, kt, qgz, sendkv, sendq, retkv, retq, ss, gs,
     xg, cxg, cpart, cret, css, cgs,
-    in_sem, send_sem, recv_sem, chunk_sem,
+    in_sem, send_sem, recv_sem, chunk_sem, mate_sem,
 ):
     lon = lax.axis_index("lon")
     lat = lax.axis_index("lat")
@@ -57,10 +57,41 @@
     ]
 
     barrier = pltpu.get_barrier_semaphore()
+    mate = lon + 1 - 2 * core
     for p in lat_peers:
-        pl.semaphore_signal(barrier, inc=1, device_id=(beside, p), device_id_type=MESH)
-    for p in lon_peers:
-        pl.semaphore_signal(barrier, inc=1, device_id=(p, lat), device_id_type=MESH)
+        pl.semaphore_signal(
+            barrier, inc=1, device_id=(beside + 1 - core, p), device_id_type=MESH
+        )
+    for dy in (2, 1, 3, 0):
+        for dx in (1, 0):
+            chip = lax.rem(y + dy, 4) * 4 + (x_lo if dx == 0 else 1 - x_lo) * 2
+            if (dy, dx) != (0, 0):
+                pl.semaphore_signal(barrier, inc=1, device_id=(chip, lat), device_id_type=MESH)
+            else:
+
+                @pl.when(core == 1)
+                def _():
+                    pl.semaphore_signal(barrier, inc=1, device_id=(mate, lat), device_id_type=MESH)
+
+    def lon_group_entered():
+        @pl.when(core == 0)
+        def _():
+            pl.semaphore_wait(barrier, GROUP - 1)
+            pl.semaphore_signal(mate_sem.at[0], inc=1, device_id=(mate, lat), device_id_type=MESH)
+
+        @pl.when(core == 1)
+        def _():
+            pl.semaphore_wait(mate_sem.at[0], 1)
+
+    def columns_entered():
+        @pl.when(core == 1)
+        def _():
+            pl.semaphore_wait(barrier, 2 * GROUP)
+            pl.semaphore_signal(mate_sem.at[1], inc=1, device_id=(mate, lat), device_id_type=MESH)
+
+        @pl.when(core == 0)
+        def _():
+            pl.semaphore_wait(mate_sem.at[1], 1)
 
     def task(ref, p, rows):
         return ref.at[lax.rem(p, 4), pl.ds(pl.multiple_of(lax.div(p, 4) * rows, rows), rows)]
@@ -187,12 +218,19 @@
                 [q[:, h * 64 : h * 64 + 64], g_row[:, h * 64 : h * 64 + 64]], axis=1
             ).astype(BF)
 
+    early = z_lat < 4
+
+    def send_rows():
+        to_tasks(2, skv, rkv, recv_sem.at[2])
+        to_tasks(3, sqg, rqg, chunk_sem.at[y])
+
     front_row()
-    pl.semaphore_wait(barrier, 2 * GROUP - 1)
-    to_tasks(2, skv, rkv, recv_sem.at[2])
-    to_tasks(3, sqg, rqg, chunk_sem.at[y])
+    lon_group_entered()
+    pl.when(early)(send_rows)
+    columns_entered()
     over_lat(0, xg.at[0], cxg.at[0], 48)
     over_lat(1, xg.at[1], cxg.at[1], 48)
+    pl.when(jnp.logical_not(early))(send_rows)
     def fold(a, op):
         out = a[:8]
         for r in range(8, a.shape[0], 8):
@@ -326,10 +364,19 @@
             from_tasks(5, sendq, retq, 32, lon_peers[4 * ((2, 1, 3, 0).index(dy)) :][:4])
         pltpu.make_async_copy(block(sendq, lon, 32), task(retq, lon, 32), recv_sem.at[5]).start()
 
-    columns(0, 0, 4)
-    stats = row_stats()
-    row_grads(stats)
-    columns(1, 1, 7)
+    rows_at = jnp.where(early, 0, 1)
+
+    @pl.loop(0, 2)
+    def _(i):
+        @pl.when(i == rows_at)
+        def _():
+            row_grads(row_stats())
+
+        @pl.when(i != rows_at)
+        def _():
+            columns(0, 0, 4)
+            columns(1, 1, 7)
+
 
     def home(a):
         return lax.dot_general(
@@ -401,7 +448,7 @@
             vm(2, 128, 512, dtype=F32), vm(2, 128, 512, dtype=F32),
             pltpu.SemaphoreType.DMA((4,)),
             pltpu.SemaphoreType.DMA((8,)), pltpu.SemaphoreType.DMA((8,)),
-            pltpu.SemaphoreType.DMA((4,)),
+            pltpu.SemaphoreType.DMA((4,)), pltpu.SemaphoreType.REGULAR((2,)),
         ],
         compiler_params=pltpu.CompilerParams(
             collective_id=0, has_side_effects=True, vmem_limit_bytes=40 * 2**20

time: 35.3 us -> 32.6 us (0.924)
  Pallas kernels: 34.4 us -> 31.7 us
    pallas_call x1, Pallas kernels: 34.4 us -> 31.7 us  [per_device(): pl.pallas_call(kernel, out_shape=jax.ShapeDtypeStruct((256, 512), BF), in...]
where the time goes in v5:
time: 32.6 us; the launch traced here: 32.5 us
  Pallas kernels  31.7 us (97%)
  local copies, waits for them, and re-layouts  0.77 us (2%)
    pallas_call x1, Pallas kernels, per_device(): pl.pallas_call(kernel, out_shape=jax.ShapeDtypeStruct((256, 512), BF), in...  31.7 us
    reshape x1, local copies, waits for them, and re-layouts, per_device(): return out.reshape(shape)  0.77 us

profile of v5, /device:TPU:1, one launch (start us, length us, event | category | flops | bytes accessed | tf_op | source)
XLA Modules:
  0.0 32.5 jit_solution(14993023090293625909)
XLA Ops:
  0.0 31.7 %axial_grads.1 = bf16[256,512]{1,0:T(8,128)(2,1)S(1)} custom-call(bf16[1024,128]{1,0:T(8,128)(2,1)} %bitcast.10, bf16[512,1536]{1,0:T(8,128)(2,1)} %w_hbm.1, bf16[512,512]{1,0:T(8,128)(2,1)} %wo_hbm.1, bf16[1024,128]{1,0:T(8,128)(2,1)} %bitcast.11), custom_call_target="tpu_custom_call" | custom-call | tf_op jit(solution)/shard_map/axial_grads/pallas_call | solution.py:435
  31.7 0.8 %reshape.19 = bf16[64,4,512]{2,1,0:T(4,128)(2,1)} reshape(bf16[256,512]{1,0:T(8,128)(2,1)S(1)} %axial_grads.1) | data formatting | bytes 524288 | tf_op jit(solution)/shard_map/reshape | solution.py:461

commit v6 on v5

--- a/solution.py
+++ b/solution.py
@@ -220,17 +220,24 @@
 
     early = z_lat < 4
 
-    def send_rows():
+    front_row()
+    lon_group_entered()
+    @pl.when(early)
+    def _():
         to_tasks(2, skv, rkv, recv_sem.at[2])
         to_tasks(3, sqg, rqg, chunk_sem.at[y])
 
-    front_row()
-    lon_group_entered()
-    pl.when(early)(send_rows)
+    @pl.when(jnp.logical_not(early))
+    def _():
+        to_tasks(2, skv, rkv, recv_sem.at[2])
+
     columns_entered()
     over_lat(0, xg.at[0], cxg.at[0], 48)
     over_lat(1, xg.at[1], cxg.at[1], 48)
-    pl.when(jnp.logical_not(early))(send_rows)
+    @pl.when(jnp.logical_not(early))
+    def _():
+        to_tasks(3, sqg, rqg, chunk_sem.at[y])
+
     def fold(a, op):
         out = a[:8]
         for r in range(8, a.shape[0], 8):
@@ -383,34 +390,46 @@
             perm[2], a, (((0,), (0,)), ((), ())), preferred_element_type=F32
         ).astype(BF)
 
-    arrived(4, cret.at[0])
-    arrived(7, cret.at[1])
-    back = [cret[half].astype(F32) for half in range(2)]
-    total = jnp.concatenate(
-        [
-            jnp.concatenate(
-                [
-                    back[half][p * 32 + t * 8 : p * 32 + t * 8 + 8]
-                    for p in range(GROUP)
-                    for half in range(2)
-                ],
-                axis=0,
-            )
-            for t in range(4)
-        ],
-        axis=1,
-    )
-    arrived(6, retkv)
-    total += dot(home(jnp.concatenate([retkv[h] for h in range(4)], axis=1)), wkv[...], NT)
-    arrived(5, retq)
-    halves = [
-        jnp.concatenate([retq[h][:, k * 64 : k * 64 + 64] for h in range(4)], axis=1)
-        for k in range(2)
-    ]
-    dq = jnp.concatenate(
-        [halves[k][la * 32 : la * 32 + 32] for la in range(4) for k in range(2)], axis=0
-    )
-    out_ref[...] = (total + dot(home(dq), w[:, :256], NT)).astype(BF)
+    def column_result():
+        arrived(4, cret.at[0])
+        arrived(7, cret.at[1])
+        back = [cret[half].astype(F32) for half in range(2)]
+        return jnp.concatenate(
+            [
+                jnp.concatenate(
+                    [
+                        back[half][p * 32 + t * 8 : p * 32 + t * 8 + 8]
+                        for p in range(GROUP)
+                        for half in range(2)
+                    ],
+                    axis=0,
+                )
+                for t in range(4)
+            ],
+            axis=1,
+        )
+
+    def row_result(first):
+        arrived(6, retkv)
+        first += dot(home(jnp.concatenate([retkv[h] for h in range(4)], axis=1)), wkv[...], NT)
+        arrived(5, retq)
+        halves = [
+            jnp.concatenate([retq[h][:, k * 64 : k * 64 + 64] for h in range(4)], axis=1)
+            for k in range(2)
+        ]
+        dq = jnp.concatenate(
+            [halves[k][la * 32 : la * 32 + 32] for la in range(4) for k in range(2)], axis=0
+        )
+        return first + dot(home(dq), w[:, :256], NT)
+
+    @pl.when(early)
+    def _():
+        total = row_result(0.0)
+        out_ref[...] = (total + column_result()).astype(BF)
+
+    @pl.when(jnp.logical_not(early))
+    def _():
+        out_ref[...] = row_result(column_result()).astype(BF)
 
     sent(0, cxg.at[0])
     sent(1, cxg.at[1])

time: 32.6 us -> 31.9 us (0.979)
  Pallas kernels: 31.7 us -> 31 us
    pallas_call x1, Pallas kernels: 31.7 us -> 31 us  [per_device(): pl.pallas_call(kernel, out_shape=jax.ShapeDtypeStruct((256, 512), BF), in...]
where the time goes in v6:
time: 31.9 us; the launch traced here: 31.8 us
  Pallas kernels  31 us (97%)
  local copies, waits for them, and re-layouts  0.77 us (2%)
    pallas_call x1, Pallas kernels, per_device(): pl.pallas_call(kernel, out_shape=jax.ShapeDtypeStruct((256, 512), BF), in...  31 us
    reshape x1, local copies, waits for them, and re-layouts, per_device(): return out.reshape(shape)  0.77 us

profile of v6, /device:TPU:1, one launch (start us, length us, event | category | flops | bytes accessed | tf_op | source)
XLA Modules:
  0.0 31.8 jit_solution(1588582268360461347)
XLA Ops:
  0.0 31.0 %axial_grads.1 = bf16[256,512]{1,0:T(8,128)(2,1)S(1)} custom-call(bf16[1024,128]{1,0:T(8,128)(2,1)} %bitcast.10, bf16[512,1536]{1,0:T(8,128)(2,1)} %w_hbm.1, bf16[512,512]{1,0:T(8,128)(2,1)} %wo_hbm.1, bf16[1024,128]{1,0:T(8,128)(2,1)} %bitcast.11), custom_call_target="tpu_custom_call" | custom-call | tf_op jit(solution)/shard_map/axial_grads/pallas_call | solution.py:454
  31.0 0.8 %reshape.19 = bf16[64,4,512]{2,1,0:T(4,128)(2,1)} reshape(bf16[256,512]{1,0:T(8,128)(2,1)S(1)} %axial_grads.1) | data formatting | bytes 524288 | tf_op jit(solution)/shard_map/reshape | solution.py:480

commit v7 on v6

--- a/solution.py
+++ b/solution.py
@@ -42,7 +42,7 @@
 
     z_lat = lax.rem(lat, 8)
     lat_peers = [
-        x_hi * 8 + lax.rem(z_lat + dz, 8) for dz in (4, 3, 5, 2, 6, 1, 7, 0) for x_hi in (0, 1)
+        x_hi * 8 + lax.rem(z_lat + dz, 8) for x_hi in (0, 1) for dz in (4, 3, 5, 2, 6, 1, 7, 0)
     ]
     y, x_lo, core = lax.div(lon, 4), lax.rem(lax.div(lon, 2), 2), lax.rem(lon, 2)
     beside = y * 4 + (1 - x_lo) * 2 + core

time: 31.9 us -> 31 us (0.972)
  Pallas kernels: 31 us -> 30.1 us
    pallas_call x1, Pallas kernels: 31 us -> 30.1 us  [per_device(): pl.pallas_call(kernel, out_shape=jax.ShapeDtypeStruct((256, 512), BF), in...]
where the time goes in v7:
time: 31 us; the launch traced here: 30.9 us
  Pallas kernels  30.1 us (97%)
  local copies, waits for them, and re-layouts  0.77 us (2%)
    pallas_call x1, Pallas kernels, per_device(): pl.pallas_call(kernel, out_shape=jax.ShapeDtypeStruct((256, 512), BF), in...  30.1 us
    reshape x1, local copies, waits for them, and re-layouts, per_device(): return out.reshape(shape)  0.77 us

profile of v7, /device:TPU:1, one launch (start us, length us, event | category | flops | bytes accessed | tf_op | source)
XLA Modules:
  0.0 30.9 jit_solution(10130004437298164977)
XLA Ops:
  0.0 30.1 %axial_grads.1 = bf16[256,512]{1,0:T(8,128)(2,1)S(1)} custom-call(bf16[1024,128]{1,0:T(8,128)(2,1)} %bitcast.10, bf16[512,1536]{1,0:T(8,128)(2,1)} %w_hbm.1, bf16[512,512]{1,0:T(8,128)(2,1)} %wo_hbm.1, bf16[1024,128]{1,0:T(8,128)(2,1)} %bitcast.11), custom_call_target="tpu_custom_call" | custom-call | tf_op jit(solution)/shard_map/axial_grads/pallas_call | solution.py:454
  30.1 0.8 %reshape.19 = bf16[64,4,512]{2,1,0:T(4,128)(2,1)} reshape(bf16[256,512]{1,0:T(8,128)(2,1)S(1)} %axial_grads.1) | data formatting | bytes 524288 | tf_op jit(solution)/shard_map/reshape | solution.py:480

commit v8 on v7

--- a/solution.py
+++ b/solution.py
@@ -254,11 +254,11 @@
             s_ref[t * size : t * size + size] = s
             top = fold(s, jnp.maximum)
             peak = top if peak is None else jnp.maximum(peak, top)
-        peak = jnp.max(peak, axis=0, keepdims=True) * EXP_SCALE
+        peak = jnp.max(peak, axis=0, keepdims=True)
         total = inner_sum = jnp.zeros((8, qz.shape[0]), F32)
         for t in range(tiles):
             at = slice(t * size, t * size + size)
-            p = jnp.exp2(s_ref[at] * EXP_SCALE - peak)
+            p = jnp.exp2((s_ref[at] - peak) * EXP_SCALE)
             gp = dot(value(t), gz, NT)
             s_ref[at] = p
             g_ref[at] = gp

time: 31 us -> 30.8 us (level)
  no operation moved by 1% of the time
where the time goes in v8:
time: 30.8 us; the launch traced here: 30.7 us
  Pallas kernels  29.9 us (97%)
  local copies, waits for them, and re-layouts  0.77 us (2%)
    pallas_call x1, Pallas kernels, per_device(): pl.pallas_call(kernel, out_shape=jax.ShapeDtypeStruct((256, 512), BF), in...  29.9 us
    reshape x1, local copies, waits for them, and re-layouts, per_device(): return out.reshape(shape)  0.77 us

profile of v8, /device:TPU:1, one launch (start us, length us, event | category | flops | bytes accessed | tf_op | source)
XLA Modules:
  0.0 30.7 jit_solution(7958954651083203840)
XLA Ops:
  0.0 29.9 %axial_grads.1 = bf16[256,512]{1,0:T(8,128)(2,1)S(1)} custom-call(bf16[1024,128]{1,0:T(8,128)(2,1)} %bitcast.10, bf16[512,1536]{1,0:T(8,128)(2,1)} %w_hbm.1, bf16[512,512]{1,0:T(8,128)(2,1)} %wo_hbm.1, bf16[1024,128]{1,0:T(8,128)(2,1)} %bitcast.11), custom_call_target="tpu_custom_call" | custom-call | tf_op jit(solution)/shard_map/axial_grads/pallas_call | solution.py:454
  30.0 0.8 %reshape.19 = bf16[64,4,512]{2,1,0:T(4,128)(2,1)} reshape(bf16[256,512]{1,0:T(8,128)(2,1)S(1)} %axial_grads.1) | data formatting | bytes 524288 | tf_op jit(solution)/shard_map/reshape | solution.py:480

commit v9 on v8

--- a/solution.py
+++ b/solution.py
@@ -32,13 +32,6 @@
     lat = lax.axis_index("lat")
     my_l = lax.div(lon, 4)
     my_h = lax.rem(lon, 4)
-
-    loads = [
-        pltpu.make_async_copy(src, dst, in_sem.at[i])
-        for i, (src, dst) in enumerate(((x_hbm, x), (c_hbm, cot), (wo_hbm, wo), (w_hbm, w)))
-    ]
-    for load in loads:
-        load.start()
 
     z_lat = lax.rem(lat, 8)
     lat_peers = [
@@ -73,6 +66,13 @@
                 def _():
                     pl.semaphore_signal(barrier, inc=1, device_id=(mate, lat), device_id_type=MESH)
 
+    loads = [
+        pltpu.make_async_copy(src, dst, in_sem.at[i])
+        for i, (src, dst) in enumerate(((x_hbm, x), (c_hbm, cot), (wo_hbm, wo), (w_hbm, w)))
+    ]
+    for load in loads:
+        load.start()
+
     def lon_group_entered():
         @pl.when(core == 0)
         def _():
@@ -99,8 +99,8 @@
     def block(ref, p, rows):
         return ref.at[pl.ds(pl.multiple_of(p * rows, rows), rows)]
 
-    def over_lat(i, src, dst, rows):
-        for p in lat_peers:
+    def over_lat(i, src, dst, rows, peers):
+        for p in peers:
             pltpu.make_async_remote_copy(
                 src_ref=block(src, p, rows),
                 dst_ref=block(dst, lat, rows),
@@ -232,8 +232,8 @@
         to_tasks(2, skv, rkv, recv_sem.at[2])
 
     columns_entered()
-    over_lat(0, xg.at[0], cxg.at[0], 48)
-    over_lat(1, xg.at[1], cxg.at[1], 48)
+    over_lat(0, xg.at[0], cxg.at[0], 48, lat_peers)
+    over_lat(1, xg.at[1], cxg.at[1], 48, lat_peers)
     @pl.when(jnp.logical_not(early))
     def _():
         to_tasks(3, sqg, rqg, chunk_sem.at[y])
@@ -319,7 +319,7 @@
             cpart[half, p * 32 : p * 32 + 32, :] = jnp.concatenate(
                 [part[p * 8 : p * 8 + 8, t * 128 : t * 128 + 128] for t in range(4)], axis=0
             ).astype(BF)
-        over_lat(i_out, cpart.at[half], cret.at[half], 32)
+        over_lat(i_out, cpart.at[half], cret.at[half], 32, range(GROUP))
 
     def chunk_rows(dy, size):
         return pl.ds(pl.multiple_of(lax.rem(y + dy, 4) * size, size), size)

time: 30.8 us -> 30.6 us (level)
  no operation moved by 1% of the time
where the time goes in v9:
time: 30.6 us; the launch traced here: 30.5 us
  Pallas kernels  29.7 us (97%)
  local copies, waits for them, and re-layouts  0.77 us (3%)
    pallas_call x1, Pallas kernels, per_device(): pl.pallas_call(kernel, out_shape=jax.ShapeDtypeStruct((256, 512), BF), in...  29.7 us
    reshape x1, local copies, waits for them, and re-layouts, per_device(): return out.reshape(shape)  0.77 us

profile of v9, /device:TPU:1, one launch (start us, length us, event | category | flops | bytes accessed | tf_op | source)
XLA Modules:
  0.0 30.5 jit_solution(6132827017426027932)
XLA Ops:
  0.0 29.7 %axial_grads.1 = bf16[256,512]{1,0:T(8,128)(2,1)S(1)} custom-call(bf16[1024,128]{1,0:T(8,128)(2,1)} %bitcast.10, bf16[512,1536]{1,0:T(8,128)(2,1)} %w_hbm.1, bf16[512,512]{1,0:T(8,128)(2,1)} %wo_hbm.1, bf16[1024,128]{1,0:T(8,128)(2,1)} %bitcast.11), custom_call_target="tpu_custom_call" | custom-call | tf_op jit(solution)/shard_map/axial_grads/pallas_call | solution.py:454
  29.7 0.8 %reshape.19 = bf16[64,4,512]{2,1,0:T(4,128)(2,1)} reshape(bf16[256,512]{1,0:T(8,128)(2,1)S(1)} %axial_grads.1) | data formatting | bytes 524288 | tf_op jit(solution)/shard_map/reshape | solution.py:480

commit v10 on v8

--- a/solution.py
+++ b/solution.py
@@ -321,14 +321,16 @@
             ).astype(BF)
         over_lat(i_out, cpart.at[half], cret.at[half], 32)
 
-    def chunk_rows(dy, size):
-        return pl.ds(pl.multiple_of(lax.rem(y + dy, 4) * size, size), size)
-
-    def row_stats():
+    def row_keys():
         arrived(2, rkv)
         keys_t = rkv[...].astype(F32).T[:64].astype(BF)
         for t in range(4):
             kt[t] = keys_t[:, t * 256 : t * 256 + 256]
+
+    def chunk_rows(dy, size):
+        return pl.ds(pl.multiple_of(lax.rem(y + dy, 4) * size, size), size)
+
+    def row_stats():
         stats = []
         for c, dy in enumerate((0, 1, 3, 2)):
             rows = rqg.at[chunk_rows(dy, 256)]
@@ -377,11 +379,13 @@
     def _(i):
         @pl.when(i == rows_at)
         def _():
+            pl.when(early)(row_keys)
             row_grads(row_stats())
 
         @pl.when(i != rows_at)
         def _():
             columns(0, 0, 4)
+            pl.when(jnp.logical_not(early))(row_keys)
             columns(1, 1, 7)
 
 

time: 30.8 us -> 30.8 us (level)
  no operation moved by 1% of the time
where the time goes in v10:
time: 30.8 us; the launch traced here: 30.7 us
  Pallas kernels  29.9 us (97%)
  local copies, waits for them, and re-layouts  0.77 us (2%)
    pallas_call x1, Pallas kernels, per_device(): pl.pallas_call(kernel, out_shape=jax.ShapeDtypeStruct((256, 512), BF), in...  29.9 us
    reshape x1, local copies, waits for them, and re-layouts, per_device(): return out.reshape(shape)  0.77 us

profile of v10, /device:TPU:1, one launch (start us, length us, event | category | flops | bytes accessed | tf_op | source)
XLA Modules:
  0.0 30.7 jit_solution(11835359368771871671)
XLA Ops:
  0.0 29.9 %axial_grads.1 = bf16[256,512]{1,0:T(8,128)(2,1)S(1)} custom-call(bf16[1024,128]{1,0:T(8,128)(2,1)} %bitcast.10, bf16[512,1536]{1,0:T(8,128)(2,1)} %w_hbm.1, bf16[512,512]{1,0:T(8,128)(2,1)} %wo_hbm.1, bf16[1024,128]{1,0:T(8,128)(2,1)} %bitcast.11), custom_call_target="tpu_custom_call" | custom-call | tf_op jit(solution)/shard_map/axial_grads/pallas_call | solution.py:458
  29.9 0.8 %reshape.19 = bf16[64,4,512]{2,1,0:T(4,128)(2,1)} reshape(bf16[256,512]{1,0:T(8,128)(2,1)S(1)} %axial_grads.1) | data formatting | bytes 524288 | tf_op jit(solution)/shard_map/reshape | solution.py:484
